TPU v7x, 32 devices: a whole 2x2x4 slice. The times are simulated.
32 devices in a mesh: mesh: 2 (over y), seq: 4 (over x, core), fsdp: 4 (over z).
Axes of the slice: x: 2, y: 2, z: 4, core: 2. Of those that a mesh axis runs over, the one named last changes fastest.
Arguments:
- latents: bfloat16 [4, 512, 5120], P('fsdp', 'mesh'), may hold values from -8 to 8
- noise: bfloat16 [4, 512, 5120], P('fsdp', 'mesh'), may hold values from -6 to 6
- noise_level: float32 [4], P('fsdp'), may hold values from 0.05 to 0.3
- group_index: int32 [4, 512], P('fsdp'), may hold values from 0 to 7, never falling along the last dimension, each value on 1 to 128 neighbouring positions
- projections: bfloat16 [2, 5120, 3, 3072], P('mesh', 'fsdp', None, 'seq'), may hold values from -1 to 1, as said below
- upstream: bfloat16 [4, 512, 3072], P('fsdp', None, 'seq'), may hold values from -0.29882812 to 0.29882812
Outputs:
- direction: bfloat16 [4, 512, 3072], P('fsdp', ('mesh', 'seq'))
- fake_grads: float32 [5120, 3, 3072], P(('mesh', 'fsdp'), None, 'seq')
Inputs may be any that keep to these rules, and one draw needn't show every extreme that they name: `projections`: along the third dimension: query, key and value projection, in that order. `group_index`: along each clip the group numbers never fall; each of the 8 groups holds 1 to 128 tokens.
All inputs are finite; a program needn't handle non-finite values.
Results may differ from a plain program's by a relative error of at most 0.018.
Values may be sent and summed in bfloat16 or wider, within the bound.
No kernel may reach another device: no remote copies, remote signals or barrier semaphores. Data moves between devices by JAX's collectives and lax.ppermute only.
A program may use at most 128 MiB of HBM per device.

v0:
```python
import math

import jax
import jax.numpy as jnp
from jax import lax
from jax.experimental import pallas as pl
from jax.experimental.pallas import tpu as pltpu
from jax.sharding import PartitionSpec as P

HEAD = 128


def shifted_by(value, axis, d, inner=1, outer=1):
    pairs = []
    for i in range(lax.axis_size(axis)):
        place = i // inner % outer
        pairs.append((i + ((place + d) % outer - place) * inner, i))
    return lax.ppermute(value, axis, pairs)


def spread(value, axis, inner, outer, at):
    pieces = [value] + [shifted_by(value, axis, d, inner, outer) for d in range(1, outer)]
    return jnp.stack(pieces, axis=at)


def turned(value, at, start):
    size = value.shape[at]
    return lax.dynamic_slice_in_dim(jnp.concatenate([value, value], axis=at), start, size, at)


def own_order(value, factors, back=False):
    sizes = [size for size, _ in factors]
    parts = value.reshape(sizes + [-1] + list(value.shape[1:]))
    for at, (size, place) in enumerate(factors):
        parts = turned(parts, at, size - place if back else place)
    return parts.reshape(value.shape)


def gather_step(step, pair, sides, chips, cores):
    first, second = pair
    if step == 0:
        return spread(first, "mesh", 1, sides, 1), spread(second, "seq", cores, chips, 1)
    if step == 1:
        return spread(first, "seq", cores, chips, 2), spread(second, "mesh", 1, sides, 1)
    both = spread(jnp.stack([first, second]), "seq", 1, cores, 4)
    both = both.reshape(2, -1, both.shape[-1])
    return both[0], both[1]


def dots(left, right, dims):
    return lax.dot_general(left, right, (dims, ((), ())), preferred_element_type=jnp.float32)


def attention_kernel(
    block, sides, side_ref, kept_ref, swapped_ref, up_ref, key_group_ref, group_ref,
    direction_ref, cot_ref, teacher_ref, fake_ref, key_grad_ref, value_grad_ref,
):
    length = kept_ref.shape[2]
    span = length // sides
    score_scale = 1.0 / math.sqrt(HEAD)
    first_side = side_ref[0] == 0
    for at in range(sides):
        here = pl.ds(at * span, span)
        there = pl.ds((sides - 1 - at) * span, span)
        kept, swapped = kept_ref[:, 0, here, :], swapped_ref[:, 0, there, :]
        teacher_ref[:, here, :] = jnp.where(first_side, kept, swapped)
        fake_ref[:, here, :] = jnp.where(first_side, swapped, kept)

    def softmax(triple_ref, rows, visible):
        scores = dots(triple_ref[0, rows, :], triple_ref[1], ((1,), (1,)))
        scores = jnp.where(visible, scores * score_scale, jnp.float32(-1e30))
        weights = jnp.exp(scores - jnp.max(scores, axis=-1, keepdims=True))
        return weights * (1.0 / jnp.sum(weights, axis=-1, keepdims=True))

    for start in range(0, length, block):
        rows = pl.ds(start, block)
        visible = key_group_ref[0, :1, :] <= group_ref[0, rows, :1]
        prob_low = softmax(teacher_ref, rows, visible).astype(jnp.bfloat16)
        teacher_out = dots(prob_low, teacher_ref[2], ((1,), (0,))).astype(jnp.bfloat16)
        probabilities = softmax(fake_ref, rows, visible)
        prob_low = probabilities.astype(jnp.bfloat16)
        values = fake_ref[2]
        fake_out = dots(prob_low, values, ((1,), (0,))).astype(jnp.bfloat16)
        direction_ref[0, rows, :] = (
            fake_out.astype(jnp.float32) - teacher_out.astype(jnp.float32)
        ).astype(jnp.bfloat16)
        grad_out = up_ref[0, rows, :]
        prob_grad = dots(grad_out, values, ((1,), (1,)))
        row_inner = jnp.sum(probabilities * prob_grad, axis=-1, keepdims=True)
        score_grad = probabilities * (prob_grad - row_inner) * score_scale
        query_grad = dots(score_grad.astype(jnp.bfloat16), fake_ref[1], ((1,), (0,)))
        cot_ref[0, 0, rows, :] = query_grad.astype(jnp.bfloat16)
        score_grad = jnp.transpose(score_grad).astype(jnp.bfloat16)
        key_part = dots(score_grad, fake_ref[0, rows, :], ((1,), (0,)))
        prob_low = jnp.transpose(probabilities).astype(jnp.bfloat16)
        value_part = dots(prob_low, grad_out, ((1,), (0,)))
        if start == 0:
            key_grad_ref[...] = key_part
            value_grad_ref[...] = value_part
        else:
            key_grad_ref[...] += key_part
            value_grad_ref[...] += value_part
    cot_ref[1, 0] = key_grad_ref[...].astype(jnp.bfloat16)
    cot_ref[2, 0] = value_grad_ref[...].astype(jnp.bfloat16)


def attention(side, sides, kept, swapped, grad_out, groups):
    _, clips, length, _ = kept.shape
    block = math.gcd(length, 256)
    area = clips * length * length

    def spec(rows, columns):
        return pl.BlockSpec((1, rows, columns), lambda clip: (clip, 0, 0))

    triple = pl.BlockSpec((3, 1, length, HEAD), lambda clip: (0, clip, 0, 0))
    return pl.pallas_call(
        lambda *refs: attention_kernel(block, sides, *refs),
        grid=(clips,),
        in_specs=[
            pl.BlockSpec(memory_space=pltpu.SMEM),
            triple, triple, spec(length, HEAD), spec(8, length), spec(length, HEAD),
        ],
        out_specs=[spec(length, HEAD), triple],
        out_shape=[
            jax.ShapeDtypeStruct((clips, length, HEAD), jnp.bfloat16),
            jax.ShapeDtypeStruct((3, clips, length, HEAD), jnp.bfloat16),
        ],
        scratch_shapes=[pltpu.VMEM((3, length, HEAD), jnp.bfloat16)] * 2
        + [pltpu.VMEM((length, HEAD), jnp.float32)] * 2,
        compiler_params=pltpu.CompilerParams(vmem_limit_bytes=60 * 1024 * 1024),
        cost_estimate=pl.CostEstimate(
            flops=18 * area * HEAD,
            bytes_accessed=20 * clips * length * HEAD,
            transcendentals=2 * area,
        ),
        name="attention",
    )(side.reshape(1), kept, swapped, grad_out, *groups)


def per_device(latents, noise, noise_level, group_index, projections, upstream):
    planes = lax.axis_size("fsdp")
    sides = lax.axis_size("mesh")
    lanes = lax.axis_size("seq")
    plane = lax.axis_index("fsdp")
    side = lax.axis_index("mesh")
    lane = lax.axis_index("seq")
    cores = 2 if lanes % 2 == 0 else 1
    chips = lanes // cores
    order = [(sides, side), (chips, lane // cores), (cores, lane % cores)]
    first_side = side == 0
    swap = [(0, 1), (1, 0)]

    rows, _, head_cols = projections.shape[1:]
    length = group_index.shape[1]
    heads = head_cols // HEAD
    pairs = (heads + 1) // 2
    shard_rows = rows // sides

    piece = latents.shape[1] // lanes
    own_rows = lax.dynamic_slice_in_dim(latents[0], lane * piece, piece, 0)
    own_noise = lax.dynamic_slice_in_dim(noise[0], lane * piece, piece, 0)
    noise_rate = noise_level[0]
    noised = (
        (1.0 - noise_rate) * own_rows.astype(jnp.float32)
        + noise_rate * own_noise.astype(jnp.float32)
    ).astype(jnp.bfloat16)

    def exchanged(blocks):
        found = []
        for d in range(planes):
            to = lax.rem(plane + planes - d, planes)
            block = lax.dynamic_index_in_dim(blocks, to, 1, False)
            found.append(shifted_by(block, "fsdp", d, 1, planes) if d else block)
        found = turned(jnp.stack(found), 0, planes - plane)
        return found.reshape(planes, piece, rows)

    def gathered(clips):
        found = clips[: planes // 2], clips[planes // 2 :]
        for step in range(3):
            found = gather_step(step, found, sides, chips, cores)
        return found

    tokens = jnp.concatenate(gathered(exchanged(noised.reshape(piece, planes, rows))))

    sums = []
    for j in range(pairs):
        factors = projections[0, :, :, 2 * j * HEAD : 2 * (j + 1) * HEAD]
        part = dots(tokens, factors, ((1,), (0,))).astype(jnp.bfloat16)
        part = part.reshape(planes, length, 3, -1).swapaxes(1, 2)
        sums.append(lax.psum_scatter(part, "fsdp", scatter_dimension=0, tiled=True)[0])

    tokens, noised = lax.optimization_barrier((tokens, noised))
    columns = noised.reshape(piece, sides, planes, shard_rows).swapaxes(1, 2)
    columns = jnp.concatenate(gathered(exchanged(columns)))

    own_up = own_order(upstream[0], order)
    groups = own_order(group_index[0], order)
    groups = (
        jnp.broadcast_to(groups[None, None, :], (1, 8, length)),
        jnp.broadcast_to(groups[None, :, None], (1, length, HEAD)),
    )
    directions, cots = [], []
    for j in range(pairs):
        even, odd = sums[j][:, :, :HEAD], sums[j][:, :, -HEAD:]
        kept = jnp.where(first_side, even, odd)
        swapped = lax.ppermute(jnp.where(first_side, odd, even), "mesh", swap)
        kept_head = jnp.minimum(2 * j + side, heads - 1)
        grad_out = lax.dynamic_slice_in_dim(own_up, kept_head * HEAD, HEAD, 1)
        direction, cotangents = attention(
            side, sides, kept[:, None], swapped[:, None], grad_out[None], groups
        )
        directions.append(direction[0])
        cots.append(lax.all_gather(cotangents[:, 0], "fsdp", axis=0))

    local = jnp.concatenate(directions, axis=1)
    local = local.reshape(sides, chips, cores, -1, pairs * HEAD)
    axes = [("mesh", 1, sides), ("seq", cores, chips), ("seq", 1, cores)]
    for at, (axis, inner, outer) in enumerate(axes):
        blocks = [lax.index_in_dim(local, -d % outer, at, False) for d in range(outer)]
        for d in range(1, outer):
            blocks[d] = shifted_by(blocks[d], axis, d, inner, outer)
        local = jnp.stack(blocks, axis=at)
    local = own_order(local.reshape(sides * lanes, -1, pairs * HEAD), order, back=True)
    local = local.reshape(sides, lanes, -1, pairs, HEAD)
    local = jnp.transpose(local, (2, 1, 3, 0, 4)).reshape(-1, lanes, pairs * sides, HEAD)
    direction = local[:, :, :heads].reshape(1, -1, lanes * head_cols)

    summed = jnp.zeros((3, shard_rows, head_cols), jnp.float32)
    for j in range(pairs):
        grad = None
        for clip in range(planes):
            block = columns[clip * length : (clip + 1) * length]
            product = dots(block, cots[j][clip], ((0,), (1,)))
            grad = product if grad is None else grad + product
        grad = jnp.swapaxes(grad, 0, 1).reshape(3, sides, shard_rows, HEAD)
        own_grad = jnp.where(first_side, grad[:, 0], grad[:, 1])
        sent = jnp.where(first_side, grad[:, 1], grad[:, 0]).astype(jnp.bfloat16)
        other = lax.ppermute(sent, "mesh", swap).astype(jnp.float32)
        first = jnp.where(first_side, own_grad, other)
        second = jnp.where(first_side, other, own_grad)
        both = jnp.concatenate([first, second], axis=2)[:, :, : (heads - 2 * j) * HEAD]
        summed = lax.dynamic_update_slice(summed, both, (0, 0, 2 * j * HEAD))
    return (direction, jnp.swapaxes(summed, 0, 1))


def solution(mesh):
    in_specs = (
        P("fsdp", "mesh", None),
        P("fsdp", "mesh", None),
        P("fsdp"),
        P("fsdp", None),
        P("mesh", "fsdp", None, "seq"),
        P("fsdp", None, "seq"),
    )
    out_specs = (P("fsdp", ("mesh", "seq"), None), P(("mesh", "fsdp"), None, "seq"))
    return jax.shard_map(
        per_device, mesh=mesh, in_specs=in_specs, out_specs=out_specs, check_vma=False
    )
```

profile of v0, /device:TPU:0, one launch (start us, length us, event | category | flops | bytes accessed | tf_op | source)
XLA Modules:
  0.0 425.1 jit_solution(15396300324312264363)
XLA Ops:
  11.3 5.1 %collective-permute-start = (bf16[64,1280]{1,0:T(8,128)(2,1)S(1)}, bf16[64,1280]{1,0:T(8,128)(2,1)S(1)}, u32[]{:S(2)}, u32[]{:S(2)}) collective-permute-start(bf16[64,1280]{1,0:T(8,128)(2,1)S(1)} %bitcast.426), channel_id=1, source_target_pairs={{1,0},{2,1},{3,2},{0,3},{5,4},{6,5},{7,6},{4,7},{9,8},{10,9},{11,1... | collective-permute-start | bytes 491528 | tf_op jit(solution)/shard_map/ppermute | solution.py:18
  17.6 3.4 collective-permute-done
  21.1 9.2 %collective-permute-done.1 = bf16[64,1280]{1,0:T(8,128)(2,1)S(1)} collective-permute-done((bf16[64,1280]{1,0:T(8,128)(2,1)S(1)}, bf16[64,1280]{1,0:T(8,128)(2,1)S(1)}, u32[]{:S(2)}, u32[]{:S(2)}) %collective-permute-start.1) | collective-permute-done | bytes 163872 | tf_op jit(solution)/shard_map/ppermute | solution.py:18
  30.5 1.6 collective-permute-start.3
  33.6 6.1 %collective-permute-done.3 = bf16[2,64,1280]{2,1,0:T(8,128)(2,1)S(1)} collective-permute-done((bf16[2,64,1280]{2,1,0:T(8,128)(2,1)S(1)}, bf16[2,64,1280]{2,1,0:T(8,128)(2,1)S(1)}, u32[]{:S(2)}, u32[]{:S(2)}) %collective-permute-start.3) | collective-permute-done | bytes 327712 | tf_op jit(solution)/shard_map/ppermute | solution.py:18
  39.8 1.6 collective-permute-start.4
  41.4 1.6 collective-permute-start.6
  43.0 12.1 %collective-permute-done.4 = bf16[2,2,64,1280]{3,2,0,1:T(8,128)(2,1)S(1)} collective-permute-done((bf16[2,2,64,1280]{3,2,0,1:T(8,128)(2,1)S(1)}, bf16[2,2,64,1280]{3,2,0,1:T(8,128)(2,1)S(1)}, u32[]{:S(2)}, u32[]{:S(2)}) %collective-permute-start.4) | collective-permute-done | bytes 655392 | tf_op jit(solution)/shard_map/ppermute | solution.py:18
  57.0 4.9 %collective-permute-done.7 = bf16[2,2,2,2,64,1280]{5,4,1,3,2,0:T(8,128)(2,1)S(1)} collective-permute-done((bf16[2,2,2,2,64,1280]{5,4,1,3,2,0:T(8,128)(2,1)S(1)}, bf16[2,2,2,2,64,1280]{5,4,1,3,2,0:T(8,128)(2,1)S(1)}, u32[]{:S(2)}, u32[]{:S(2)}) %collective-permute-start.7) | collective-permute-done | bytes 2621472 | tf_op jit(solution)/shard_map/ppermute | solution.py:18
  62.9 8.9 %fusion.12 = bf16[2048,3,256]{2,0,1:T(8,128)(2,1)S(1)} fusion(bf16[1,1280,3,768]{3,1,2,0:T(8,128)(2,1)} %param.10, bf16[1024,1280]{1,0:T(8,128)(2,1)S(1)} %bitcast.384, bf16[1024,1280]{1,0:T(8,128)(2,1)S(1)} %bitcast.381), kind=kOutput, calls=%fused_computation.19 | convolution fusion | flops 4038590464 | bytes 10354688 | tf_op jit(solution)/shard_map/dot_general | solution.py:51
  71.8 1.9 copy.234
  73.9 6.6 %fusion.9 = bf16[2048,3,256]{2,0,1:T(8,128)(2,1)S(1)} fusion(bf16[1,1280,3,768]{3,1,2,0:T(8,128)(2,1)} %param.10, bf16[1024,1280]{1,0:T(8,128)(2,1)} %bitcast.385, bf16[1024,1280]{1,0:T(8,128)(2,1)S(1)} %bitcast.382), kind=kOutput, calls=%fused_computation.18 | convolution fusion | flops 4038590464 | bytes 10354688 | tf_op jit(solution)/shard_map/dot_general | solution.py:51
  80.5 1.9 copy.235
  82.5 6.6 %fusion.6 = bf16[2048,3,256]{2,0,1:T(8,128)(2,1)S(1)} fusion(bf16[1,1280,3,768]{3,1,2,0:T(8,128)(2,1)} %param.10, bf16[1024,1280]{1,0:T(8,128)(2,1)} %bitcast.386, bf16[1024,1280]{1,0:T(8,128)(2,1)S(1)} %bitcast.383), kind=kOutput, calls=%fused_computation.17 | convolution fusion | flops 4038590464 | bytes 10354688 | tf_op jit(solution)/shard_map/dot_general | solution.py:51
  89.1 1.9 copy.236
  93.0 2.5 collective-permute-start.15
  96.2 2.2 collective-permute-start.16
  101.0 5.9 %collective-permute-done.14 = bf16[64,2,640]{2,0,1:T(8,128)(2,1)S(1)} collective-permute-done((bf16[64,2,640]{2,0,1:T(8,128)(2,1)S(1)}, bf16[64,2,640]{2,0,1:T(8,128)(2,1)S(1)}, u32[]{:S(2)}, u32[]{:S(2)}) %collective-permute-start.14) | collective-permute-done | bytes 163872 | tf_op jit(solution)/shard_map/ppermute | solution.py:18
  107.6 19.9 %collective-permute-done.15 = bf16[64,2,640]{2,0,1:T(8,128)(2,1)S(1)} collective-permute-done((bf16[64,2,640]{2,0,1:T(8,128)(2,1)S(1)}, bf16[64,2,640]{2,0,1:T(8,128)(2,1)S(1)}, u32[]{:S(2)}, u32[]{:S(2)}) %collective-permute-start.15) | collective-permute-done | bytes 163872 | tf_op jit(solution)/shard_map/ppermute | solution.py:18
  131.6 12.1 %reduce-scatter.8.cloned.1.call-done = bf16[1,3,512,256]{3,2,1,0:T(8,128)(2,1)} async-done(((bf16[4,3,512,256]{3,2,1,0:T(8,128)(2,1)}), bf16[1,3,512,256]{3,2,1,0:T(8,128)(2,1)}) %reduce-scatter.8.cloned.1.call-update) | async-done | bytes 786448 | tf_op jit(solution)/shard_map/reduce_scatter | solution.py:190
  143.7 1.9 broadcast_select_fusion
  152.2 5.4 %collective-permute-done.10 = bf16[3,512,128]{2,1,0:T(8,128)(2,1)S(1)} collective-permute-done((bf16[3,512,128]{2,1,0:T(8,128)(2,1)S(1)}, bf16[3,512,128]{2,1,0:T(8,128)(2,1)S(1)}, u32[]{:S(2)}, u32[]{:S(2)}) %collective-permute-start.10) | collective-permute-done | bytes 393248 | tf_op jit(solution)/shard_map/ppermute | solution.py:206
  159.1 5.0 %attention.5 = (bf16[1,512,128]{2,1,0:T(8,128)(2,1)}, bf16[3,1,512,128]{3,2,1,0:T(8,128)(2,1)}) custom-call(s32[1]{0:T(128)} %bitcast.refs_0_, bf16[3,1,512,128]{3,2,1,0:T(8,128)(2,1)} %get-tuple-element.44.refs_1_, bf16[3,1,512,128]{3,2,1,0:T(8,128)(2,1)} %bitcast.432, bf16[1,512,128]{2,1,0:T(8,128)(2,1)} %get-tuple-element.37.refs_3_, ...), custom_call_target="tpu_custom_call" | custom-call | flops 603979776 | bytes 1310720 | tf_op jit(solution)/shard_map/attention/pallas_call | solution.py:116
  169.0 10.0 %collective-permute-done.18 = bf16[2,2,64,1280]{3,2,0,1:T(8,128)(2,1)S(1)} collective-permute-done((bf16[2,2,64,1280]{3,2,0,1:T(8,128)(2,1)S(1)}, bf16[2,2,64,1280]{3,2,0,1:T(8,128)(2,1)S(1)}, u32[]{:S(2)}, u32[]{:S(2)}) %collective-permute-start.18) | collective-permute-done | bytes 655392 | tf_op jit(solution)/shard_map/ppermute | solution.py:18
  179.1 2.8 collective-permute-done.20
  182.0 1.8 pad_maximum_fusion.3
  183.8 24.7 %reduce-scatter.6.cloned.1.call-done = bf16[1,3,512,256]{3,2,1,0:T(8,128)(2,1)} async-done(((bf16[4,3,512,256]{3,2,1,0:T(8,128)(2,1)}), bf16[1,3,512,256]{3,2,1,0:T(8,128)(2,1)}) %reduce-scatter.6.cloned.1.call-update) | async-done | bytes 786448 | tf_op jit(solution)/shard_map/reduce_scatter | solution.py:190
  208.5 1.9 broadcast_select_fusion.1
  211.9 9.2 %collective-permute-done.9 = bf16[3,512,128]{2,1,0:T(8,128)(2,1)S(1)} collective-permute-done((bf16[3,512,128]{2,1,0:T(8,128)(2,1)S(1)}, bf16[3,512,128]{2,1,0:T(8,128)(2,1)S(1)}, u32[]{:S(2)}, u32[]{:S(2)}) %collective-permute-start.9) | collective-permute-done | bytes 393248 | tf_op jit(solution)/shard_map/ppermute | solution.py:206
  221.9 5.0 %attention.4 = (bf16[1,512,128]{2,1,0:T(8,128)(2,1)}, bf16[3,1,512,128]{3,2,1,0:T(8,128)(2,1)}) custom-call(s32[1]{0:T(128)} %bitcast.refs_0_, bf16[3,1,512,128]{3,2,1,0:T(8,128)(2,1)} %get-tuple-element.42.refs_1_, bf16[3,1,512,128]{3,2,1,0:T(8,128)(2,1)} %bitcast.434, bf16[1,512,128]{2,1,0:T(8,128)(2,1)} %get-tuple-element.38.refs_3_, ...), custom_call_target="tpu_custom_call" | custom-call | flops 603979776 | bytes 1310720 | tf_op jit(solution)/shard_map/attention/pallas_call | solution.py:116
  227.0 44.2 %reduce-scatter.4.cloned.1.call-done = bf16[1,3,512,256]{3,2,1,0:T(8,128)(2,1)} async-done(((bf16[4,3,512,256]{3,2,1,0:T(8,128)(2,1)}), bf16[1,3,512,256]{3,2,1,0:T(8,128)(2,1)}) %reduce-scatter.4.cloned.1.call-update) | async-done | bytes 786448 | tf_op jit(solution)/shard_map/reduce_scatter | solution.py:190
  271.1 2.0 broadcast_select_fusion.2
  274.6 9.2 %collective-permute-done.8 = bf16[3,512,128]{2,1,0:T(8,128)(2,1)S(1)} collective-permute-done((bf16[3,512,128]{2,1,0:T(8,128)(2,1)S(1)}, bf16[3,512,128]{2,1,0:T(8,128)(2,1)S(1)}, u32[]{:S(2)}, u32[]{:S(2)}) %collective-permute-start.8) | collective-permute-done | bytes 393248 | tf_op jit(solution)/shard_map/ppermute | solution.py:206
  284.5 5.0 %attention.3 = (bf16[1,512,128]{2,1,0:T(8,128)(2,1)}, bf16[3,1,512,128]{3,2,1,0:T(8,128)(2,1)}) custom-call(s32[1]{0:T(128)} %bitcast.refs_0_, bf16[3,1,512,128]{3,2,1,0:T(8,128)(2,1)} %get-tuple-element.40.refs_1_, bf16[3,1,512,128]{3,2,1,0:T(8,128)(2,1)} %bitcast.433, bf16[1,512,128]{2,1,0:T(8,128)(2,1)} %get-tuple-element.36.refs_3_, ...), custom_call_target="tpu_custom_call" | custom-call | flops 603979776 | bytes 1310720 | tf_op jit(solution)/shard_map/attention/pallas_call | solution.py:116
  292.1 4.2 collective-permute-done.11
  296.3 1.6 collective-permute-start.12
  297.9 4.2 collective-permute-done.12
  302.2 2.2 pad_maximum_fusion.4
  309.7 2.4 fusion.37
  318.5 28.7 %all-gather.9.cloned.1.call-done = bf16[12,1,512,128]{3,2,1,0:T(8,128)(2,1)} async-done(((bf16[3,1,512,128]{3,2,1,0:T(8,128)(2,1)}), bf16[12,1,512,128]{3,2,1,0:T(8,128)(2,1)}) %all-gather.9.cloned.1.call-update) | async-done | bytes 1572880 | tf_op jit(solution)/shard_map/all_gather | solution.py:213
  347.1 2.4 fusion.38
  350.4 2.2 convolution_add_fusion.4
  352.6 31.9 %all-gather.7.cloned.1.call-done = bf16[12,1,512,128]{3,2,1,0:T(8,128)(2,1)} async-done(((bf16[3,1,512,128]{3,2,1,0:T(8,128)(2,1)}), bf16[12,1,512,128]{3,2,1,0:T(8,128)(2,1)}) %all-gather.7.cloned.1.call-update) | async-done | bytes 1572880 | tf_op jit(solution)/shard_map/all_gather | solution.py:213
  384.5 2.4 fusion.39
  391.3 1.9 convolution_add_fusion.3
  393.9 10.1 %collective-permute-done.22 = bf16[3,640,128]{2,1,0:T(8,128)(2,1)S(1)} collective-permute-done((bf16[3,640,128]{2,1,0:T(8,128)(2,1)S(1)}, bf16[3,640,128]{2,1,0:T(8,128)(2,1)S(1)}, u32[]{:S(2)}, u32[]{:S(2)}) %collective-permute-start.22) | collective-permute-done | bytes 491552 | tf_op jit(solution)/shard_map/ppermute | solution.py:238
  404.6 8.6 %collective-permute-done.23 = bf16[3,640,128]{2,1,0:T(8,128)(2,1)S(1)} collective-permute-done((bf16[3,640,128]{2,1,0:T(8,128)(2,1)S(1)}, bf16[3,640,128]{2,1,0:T(8,128)(2,1)S(1)}, u32[]{:S(2)}, u32[]{:S(2)}) %collective-permute-start.23) | collective-permute-done | bytes 491552 | tf_op jit(solution)/shard_map/ppermute | solution.py:238
  415.2 2.6 copy-done.6
  (166 shorter events, 59.9 us)
Async XLA Ops:
  7.2 136.5 %reduce-scatter.8.cloned.1.call-start = ((), (), s32[]{:S(2)}) async-start(), calls=%async_computation.5 | async-start | bytes 3932160 | tf_op jit(solution)/shard_map/reduce_scatter | solution.py:190
  11.3 9.8 %collective-permute-start = (bf16[64,1280]{1,0:T(8,128)(2,1)S(1)}, bf16[64,1280]{1,0:T(8,128)(2,1)S(1)}, u32[]{:S(2)}, u32[]{:S(2)}) collective-permute-start(bf16[64,1280]{1,0:T(8,128)(2,1)S(1)} %bitcast.426), channel_id=1, source_target_pairs={{1,0},{2,1},{3,2},{0,3},{5,4},{6,5},{7,6},{4,7},{9,8},{10,9},{11,1... | collective-permute-start | bytes 491528 | tf_op jit(solution)/shard_map/ppermute | solution.py:18
  16.4 13.9 %collective-permute-start.1 = (bf16[64,1280]{1,0:T(8,128)(2,1)S(1)}, bf16[64,1280]{1,0:T(8,128)(2,1)S(1)}, u32[]{:S(2)}, u32[]{:S(2)}) collective-permute-start(bf16[64,1280]{1,0:T(8,128)(2,1)S(1)} %bitcast.427), channel_id=1, source_target_pairs={{2,0},{3,1},{0,2},{1,3},{6,4},{7,5},{4,6},{5,7},{10,8},{11,9},{8,1... | collective-permute-start | bytes 491528 | tf_op jit(solution)/shard_map/ppermute | solution.py:18
  16.5 13.8 %collective-permute-start.2 = (bf16[64,1280]{1,0:T(8,128)(2,1)S(1)}, bf16[64,1280]{1,0:T(8,128)(2,1)S(1)}, u32[]{:S(2)}, u32[]{:S(2)}) collective-permute-start(bf16[64,1280]{1,0:T(8,128)(2,1)S(1)} %bitcast.428), channel_id=1, source_target_pairs={{3,0},{0,1},{1,2},{2,3},{7,4},{4,5},{5,6},{6,7},{11,8},{8,9},{9,10... | collective-permute-start | bytes 491528 | tf_op jit(solution)/shard_map/ppermute | solution.py:18
  30.5 9.2 %collective-permute-start.3 = (bf16[2,64,1280]{2,1,0:T(8,128)(2,1)S(1)}, bf16[2,64,1280]{2,1,0:T(8,128)(2,1)S(1)}, u32[]{:S(2)}, u32[]{:S(2)}) collective-permute-start(bf16[2,64,1280]{2,1,0:T(8,128)(2,1)S(1)} %get-tuple-element.34), channel_id=1, source_target_pairs={{16,0},{0,16},{17,1},{1,17},{18,2},{2,18},{19,3},{3,19},{20,4},{4,... | collective-permute-start | bytes 983048 | tf_op jit(solution)/shard_map/ppermute | solution.py:18
  32.1 9.3 %collective-permute-start.5 = (bf16[2,64,1280]{2,1,0:T(8,128)(2,1)S(1)}, bf16[2,64,1280]{2,1,0:T(8,128)(2,1)S(1)}, u32[]{:S(2)}, u32[]{:S(2)}) collective-permute-start(bf16[2,64,1280]{2,1,0:T(8,128)(2,1)S(1)} %get-tuple-element.35), channel_id=1, source_target_pairs={{8,0},{12,4},{0,8},{4,12},{9,1},{13,5},{1,9},{5,13},{10,2},{14,6},... | collective-permute-start | bytes 983048 | tf_op jit(solution)/shard_map/ppermute | solution.py:18
  39.8 15.3 %collective-permute-start.4 = (bf16[2,2,64,1280]{3,2,0,1:T(8,128)(2,1)S(1)}, bf16[2,2,64,1280]{3,2,0,1:T(8,128)(2,1)S(1)}, u32[]{:S(2)}, u32[]{:S(2)}) collective-permute-start(bf16[2,2,64,1280]{3,2,0,1:T(8,128)(2,1)S(1)} %get-tuple-element.54), channel_id=1, source_target_pairs={{8,0},{12,4},{0,8},{4,12},{9,1},{13,5},{1,9},{5,13},{10,2},{14,6},... | collective-permute-start | bytes 1966088 | tf_op jit(solution)/shard_map/ppermute | solution.py:18
  41.4 15.0 %collective-permute-start.6 = (bf16[2,2,64,1280]{3,2,0,1:T(8,128)(2,1)S(1)}, bf16[2,2,64,1280]{3,2,0,1:T(8,128)(2,1)S(1)}, u32[]{:S(2)}, u32[]{:S(2)}) collective-permute-start(bf16[2,2,64,1280]{3,2,0,1:T(8,128)(2,1)S(1)} %get-tuple-element.56), channel_id=1, source_target_pairs={{16,0},{0,16},{17,1},{1,17},{18,2},{2,18},{19,3},{3,19},{20,4},{4,... | collective-permute-start | bytes 1966088 | tf_op jit(solution)/shard_map/ppermute | solution.py:18
  56.9 5.0 %collective-permute-start.7 = (bf16[2,2,2,2,64,1280]{5,4,1,3,2,0:T(8,128)(2,1)S(1)}, bf16[2,2,2,2,64,1280]{5,4,1,3,2,0:T(8,128)(2,1)S(1)}, u32[]{:S(2)}, u32[]{:S(2)}) collective-permute-start(bf16[2,2,2,2,64,1280]{5,4,1,3,2,0:T(8,128)(2,1)S(1)} %get-tuple-element.25), channel_id=1, source_target_pairs={{4,0},{0,4},{12,8},{8,12},{5,1},{1,5},{13,9},{9,13},{6,2},{2,6},{1... | collective-permute-start | bytes 7864328 | tf_op jit(solution)/shard_map/ppermute | solution.py:18
  62.9 8.9 %copy-start.7 = (bf16[1,2,2,2,2,64,1280]{6,5,4,3,2,1,0:T(8,128)(2,1)}, bf16[1,2,2,2,2,64,1280]{6,5,4,3,2,1,0:T(8,128)(2,1)S(1)}, u32[]{:S(2)}) copy-start(bf16[1,2,2,2,2,64,1280]{6,5,4,3,2,1,0:T(8,128)(2,1)S(1)} %copy.123) | copy-start | bytes 7864324
  73.7 134.8 %reduce-scatter.6.cloned.1.call-start = ((), (), s32[]{:S(2)}) async-start(), calls=%async_computation.4 | async-start | bytes 3932160 | tf_op jit(solution)/shard_map/reduce_scatter | solution.py:190
  82.4 188.7 %reduce-scatter.4.cloned.1.call-start = ((), (), s32[]{:S(2)}) async-start(), calls=%async_computation.3 | async-start | bytes 3932160 | tf_op jit(solution)/shard_map/reduce_scatter | solution.py:190
  91.0 218.8 %all-gather.11.cloned.1.call-start = ((), (), s32[]{:S(2)}) async-start(), calls=%async_computation.8 | async-start | bytes 1966080 | tf_op jit(solution)/shard_map/all_gather | solution.py:213
  91.5 7.4 %copy-start.14 = (s32[1,512]{1,0:T(1,128)S(1)}, s32[1,512]{1,0:T(1,128)}, u32[]{:S(2)}) copy-start(s32[1,512]{1,0:T(1,128)} %param.9) | copy-start | bytes 6148
  91.5 8.2 %copy-start.11 = (bf16[1,512,768]{2,1,0:T(8,128)(2,1)S(1)}, bf16[1,512,768]{2,1,0:T(8,128)(2,1)}, u32[]{:S(2)}) copy-start(bf16[1,512,768]{2,1,0:T(8,128)(2,1)} %param.11) | copy-start | bytes 2359300
  92.9 14.0 %collective-permute-start.14 = (bf16[64,2,640]{2,0,1:T(8,128)(2,1)S(1)}, bf16[64,2,640]{2,0,1:T(8,128)(2,1)S(1)}, u32[]{:S(2)}, u32[]{:S(2)}) collective-permute-start(bf16[64,2,640]{2,0,1:T(8,128)(2,1)S(1)} %bitcast.424), channel_id=1, source_target_pairs={{1,0},{2,1},{3,2},{0,3},{5,4},{6,5},{7,6},{4,7},{9,8},{10,9},{11,1... | collective-permute-start | bytes 491528 | tf_op jit(solution)/shard_map/ppermute | solution.py:18
  93.0 34.4 %collective-permute-start.15 = (bf16[64,2,640]{2,0,1:T(8,128)(2,1)S(1)}, bf16[64,2,640]{2,0,1:T(8,128)(2,1)S(1)}, u32[]{:S(2)}, u32[]{:S(2)}) collective-permute-start(bf16[64,2,640]{2,0,1:T(8,128)(2,1)S(1)} %bitcast.425), channel_id=1, source_target_pairs={{2,0},{3,1},{0,2},{1,3},{6,4},{7,5},{4,6},{5,7},{10,8},{11,9},{8,1... | collective-permute-start | bytes 491528 | tf_op jit(solution)/shard_map/ppermute | solution.py:18
  96.2 31.9 %collective-permute-start.16 = (bf16[64,2,640]{2,0,1:T(8,128)(2,1)}, bf16[64,2,640]{2,0,1:T(8,128)(2,1)S(1)}, u32[]{:S(2)}, u32[]{:S(2)}) collective-permute-start(bf16[64,2,640]{2,0,1:T(8,128)(2,1)} %bitcast.350), channel_id=1, source_target_pairs={{3,0},{0,1},{1,2},{2,3},{7,4},{4,5},{5,6},{6,7},{11,8},{8,9},{9,10... | collective-permute-start | bytes 491528 | tf_op jit(solution)/shard_map/ppermute | solution.py:18
  145.6 12.0 %collective-permute-start.10 = (bf16[3,512,128]{2,1,0:T(8,128)(2,1)S(1)}, bf16[3,512,128]{2,1,0:T(8,128)(2,1)S(1)}, u32[]{:S(2)}, u32[]{:S(2)}) collective-permute-start(bf16[3,512,128]{2,1,0:T(8,128)(2,1)S(1)} %get-tuple-element.43), channel_id=1, source_target_pairs={{0,16},{16,0},{1,17},{17,1},{2,18},{18,2},{3,19},{19,3},{4,20},{20... | collective-permute-start | bytes 1179656 | tf_op jit(solution)/shard_map/ppermute | solution.py:206
  148.2 16.0 %collective-permute-start.17 = (bf16[2,64,1280]{2,1,0:T(8,128)(2,1)S(1)}, bf16[2,64,1280]{2,1,0:T(8,128)(2,1)S(1)}, u32[]{:S(2)}, u32[]{:S(2)}) collective-permute-start(bf16[2,64,1280]{2,1,0:T(8,128)(2,1)S(1)} %bitcast.415), channel_id=1, source_target_pairs={{16,0},{0,16},{17,1},{1,17},{18,2},{2,18},{19,3},{3,19},{20,4},{4,... | collective-permute-start | bytes 983048 | tf_op jit(solution)/shard_map/ppermute | solution.py:18
  150.7 15.7 %collective-permute-start.19 = (bf16[2,64,1280]{2,1,0:T(8,128)(2,1)S(1)}, bf16[2,64,1280]{2,1,0:T(8,128)(2,1)}, u32[]{:S(2)}, u32[]{:S(2)}) collective-permute-start(bf16[2,64,1280]{2,1,0:T(8,128)(2,1)S(1)} %bitcast.416), channel_id=1, source_target_pairs={{8,0},{12,4},{0,8},{4,12},{9,1},{13,5},{1,9},{5,13},{10,2},{14,6},... | collective-permute-start | bytes 983048 | tf_op jit(solution)/shard_map/ppermute | solution.py:18
  157.6 1.5 copy-start.15
  164.2 183.0 %all-gather.9.cloned.1.call-start = ((), (), s32[]{:S(2)}) async-start(), calls=%async_computation.7 | async-start | bytes 1966080 | tf_op jit(solution)/shard_map/all_gather | solution.py:213
  164.3 14.7 %collective-permute-start.18 = (bf16[2,2,64,1280]{3,2,0,1:T(8,128)(2,1)S(1)}, bf16[2,2,64,1280]{3,2,0,1:T(8,128)(2,1)S(1)}, u32[]{:S(2)}, u32[]{:S(2)}) collective-permute-start(bf16[2,2,64,1280]{3,2,0,1:T(8,128)(2,1)S(1)} %get-tuple-element.46), channel_id=1, source_target_pairs={{8,0},{12,4},{0,8},{4,12},{9,1},{13,5},{1,9},{5,13},{10,2},{14,6},... | collective-permute-start | bytes 1966088 | tf_op jit(solution)/shard_map/ppermute | solution.py:18
  167.5 14.4 %collective-permute-start.20 = (bf16[2,2,64,1280]{3,2,0,1:T(8,128)(2,1)S(1)}, bf16[2,2,64,1280]{3,2,0,1:T(8,128)(2,1)S(1)}, u32[]{:S(2)}, u32[]{:S(2)}) collective-permute-start(bf16[2,2,64,1280]{3,2,0,1:T(8,128)(2,1)S(1)} %get-tuple-element.48), channel_id=1, source_target_pairs={{16,0},{0,16},{17,1},{1,17},{18,2},{2,18},{19,3},{3,19},{20,4},{4,... | collective-permute-start | bytes 1966088 | tf_op jit(solution)/shard_map/ppermute | solution.py:18
  183.8 118.4 %collective-permute-start.21 = (bf16[2,2,2,2,64,1280]{5,4,1,2,3,0:T(8,128)(2,1)}, bf16[2,2,2,2,64,1280]{5,4,1,2,3,0:T(8,128)(2,1)}, u32[]{:S(2)}, u32[]{:S(2)}) collective-permute-start(bf16[2,2,2,2,64,1280]{5,4,1,2,3,0:T(8,128)(2,1)} %get-tuple-element.22), channel_id=1, source_target_pairs={{4,0},{0,4},{12,8},{8,12},{5,1},{1,5},{13,9},{9,13},{6,2},{2,6},{1... | collective-permute-start | bytes 7864328 | tf_op jit(solution)/shard_map/ppermute | solution.py:18
  210.4 10.7 %collective-permute-start.9 = (bf16[3,512,128]{2,1,0:T(8,128)(2,1)S(1)}, bf16[3,512,128]{2,1,0:T(8,128)(2,1)S(1)}, u32[]{:S(2)}, u32[]{:S(2)}) collective-permute-start(bf16[3,512,128]{2,1,0:T(8,128)(2,1)S(1)} %get-tuple-element.41), channel_id=1, source_target_pairs={{0,16},{16,0},{1,17},{17,1},{2,18},{18,2},{3,19},{19,3},{4,20},{20... | collective-permute-start | bytes 1179656 | tf_op jit(solution)/shard_map/ppermute | solution.py:206
  221.1 0.8 copy-start.17
  226.9 157.6 %all-gather.7.cloned.1.call-start = ((), (), s32[]{:S(2)}) async-start(), calls=%async_computation.6 | async-start | bytes 1966080 | tf_op jit(solution)/shard_map/all_gather | solution.py:213
  271.1 18.4 %copy-start.12 = (bf16[1,512,128]{2,1,0:T(8,128)(2,1)S(1)}, bf16[1,512,128]{2,1,0:T(8,128)(2,1)}, u32[]{:S(2)}) copy-start(bf16[1,512,128]{2,1,0:T(8,128)(2,1)} %get-tuple-element.11) | copy-start | bytes 393220
  271.1 18.4 %copy-start.13 = (bf16[1,512,128]{2,1,0:T(8,128)(2,1)S(1)}, bf16[1,512,128]{2,1,0:T(8,128)(2,1)}, u32[]{:S(2)}) copy-start(bf16[1,512,128]{2,1,0:T(8,128)(2,1)} %get-tuple-element.10) | copy-start | bytes 393220
  273.1 10.7 %collective-permute-start.8 = (bf16[3,512,128]{2,1,0:T(8,128)(2,1)S(1)}, bf16[3,512,128]{2,1,0:T(8,128)(2,1)S(1)}, u32[]{:S(2)}, u32[]{:S(2)}) collective-permute-start(bf16[3,512,128]{2,1,0:T(8,128)(2,1)S(1)} %get-tuple-element.39), channel_id=1, source_target_pairs={{0,16},{16,0},{1,17},{17,1},{2,18},{18,2},{3,19},{19,3},{4,20},{20... | collective-permute-start | bytes 1179656 | tf_op jit(solution)/shard_map/ppermute | solution.py:206
  290.6 5.7 %collective-permute-start.11 = (bf16[2,2,64,384]{3,2,1,0:T(8,128)(2,1)S(1)}, bf16[2,2,64,384]{3,2,1,0:T(8,128)(2,1)S(1)}, u32[]{:S(2)}, u32[]{:S(2)}) collective-permute-start(bf16[2,2,64,384]{3,2,1,0:T(8,128)(2,1)S(1)} %bitcast.423), channel_id=1, source_target_pairs={{16,0},{0,16},{17,1},{1,17},{18,2},{2,18},{19,3},{3,19},{20,4},{4,... | collective-permute-start | bytes 589832 | tf_op jit(solution)/shard_map/ppermute | solution.py:18
  296.3 5.7 %collective-permute-start.12 = (bf16[2,2,64,384]{3,2,0,1:T(8,128)(2,1)S(1)}, bf16[2,2,64,384]{3,2,0,1:T(8,128)(2,1)S(1)}, u32[]{:S(2)}, u32[]{:S(2)}) collective-permute-start(bf16[2,2,64,384]{3,2,0,1:T(8,128)(2,1)S(1)} %get-tuple-element.64), channel_id=1, source_target_pairs={{8,0},{12,4},{0,8},{4,12},{9,1},{13,5},{1,9},{5,13},{10,2},{14,6},... | collective-permute-start | bytes 589832 | tf_op jit(solution)/shard_map/ppermute | solution.py:18
  302.1 5.0 %collective-permute-start.13 = (bf16[2,2,64,384]{3,2,1,0:T(8,128)(2,1)S(1)}, bf16[2,2,64,384]{3,2,1,0:T(8,128)(2,1)S(1)}, u32[]{:S(2)}, u32[]{:S(2)}) collective-permute-start(bf16[2,2,64,384]{3,2,1,0:T(8,128)(2,1)S(1)} %get-tuple-element.62), channel_id=1, source_target_pairs={{4,0},{0,4},{12,8},{8,12},{5,1},{1,5},{13,9},{9,13},{6,2},{2,6},{1... | collective-permute-start | bytes 589832 | tf_op jit(solution)/shard_map/ppermute | solution.py:18
  309.7 2.4 copy-start
  309.7 2.4 copy-start.8
  314.8 1.3 copy-start.3
  317.0 96.5 %collective-permute-start.24 = (bf16[3,640,128]{2,1,0:T(8,128)(2,1)}, bf16[3,640,128]{2,1,0:T(8,128)(2,1)S(1)}, u32[]{:S(2)}, u32[]{:S(2)}) collective-permute-start(bf16[3,640,128]{2,1,0:T(8,128)(2,1)} %fusion.33), channel_id=1, source_target_pairs={{0,16},{16,0},{1,17},{17,1},{2,18},{18,2},{3,19},{19,3},{4,20},{20... | collective-permute-start | bytes 1474568 | tf_op jit(solution)/shard_map/ppermute | solution.py:238
  347.1 2.4 copy-start.1
  347.1 2.4 copy-start.9
  384.5 2.4 copy-start.2
  384.5 2.4 copy-start.10
  388.8 2.5 copy-start.5
  389.8 14.2 %collective-permute-start.22 = (bf16[3,640,128]{2,1,0:T(8,128)(2,1)S(1)}, bf16[3,640,128]{2,1,0:T(8,128)(2,1)S(1)}, u32[]{:S(2)}, u32[]{:S(2)}) collective-permute-start(bf16[3,640,128]{2,1,0:T(8,128)(2,1)S(1)} %fusion.31), channel_id=1, source_target_pairs={{0,16},{16,0},{1,17},{17,1},{2,18},{18,2},{3,19},{19,3},{4,20},{20... | collective-permute-start | bytes 1474568 | tf_op jit(solution)/shard_map/ppermute | solution.py:238
  393.3 19.9 %collective-permute-start.23 = (bf16[3,640,128]{2,1,0:T(8,128)(2,1)S(1)}, bf16[3,640,128]{2,1,0:T(8,128)(2,1)S(1)}, u32[]{:S(2)}, u32[]{:S(2)}) collective-permute-start(bf16[3,640,128]{2,1,0:T(8,128)(2,1)S(1)} %fusion.32), channel_id=1, source_target_pairs={{0,16},{16,0},{1,17},{17,1},{2,18},{18,2},{3,19},{19,3},{4,20},{20... | collective-permute-start | bytes 1474568 | tf_op jit(solution)/shard_map/ppermute | solution.py:238
  413.4 1.5 copy-start.4
  415.2 2.6 copy-start.6
  (1 other events, 0.7 us)
Sparse Core Ops, SparseCore 0:
  73.8 69.8 reduce-scatter.7
  146.0 62.4 reduce-scatter.5
  210.8 60.2 reduce-scatter.3
  272.6 37.1 all-gather.10
  311.1 35.9 all-gather.8
  348.5 35.9 all-gather.6
where the time goes:
time: 431 us; the launch traced here: 425 us
  waiting for transfers between devices  268 us (62%)
  matrix products  39.5 us (9%)
  starting transfers between devices  34.1 us (8%)
  local copies, waits for them, and re-layouts  32.7 us (8%)
  other arithmetic  19.4 us (5%)
  between operations  16 us (4%)
  Pallas kernels  15 us (3%)
    ppermute x19, waiting for transfers between devices, shifted_by(): return lax.ppermute(value, axis, pairs)  83.9 us
    reduce_scatter x3, waiting for transfers between devices, per_device(): lax.psum_scatter(part, 'fsdp', scatter_dimension=0, tiled=True)[0]  81 us
    all_gather x3, waiting for transfers between devices, per_device(): cots.append(lax.all_gather(cotangents[:, 0], 'fsdp', axis=0))  60.8 us
    dot_general x15, matrix products, dots(): lax.dot_general(left, right, (dims, ((), ())), preferred_element_type=jnp...  39.5 us
    ppermute x19, starting transfers between devices, shifted_by(): return lax.ppermute(value, axis, pairs)  25.6 us
    ppermute x3, waiting for transfers between devices, per_device(): swapped = lax.ppermute(jnp.where(first_side, odd, even), 'mesh', swap)  23.8 us
    ppermute x3, waiting for transfers between devices, per_device(): other = lax.ppermute(sent, 'mesh', swap).astype(jnp.float32)  18.7 us
    pallas_call x3, Pallas kernels, attention(): pl.pallas_call(lambda *refs: attention_kernel(block, sides, *refs), grid=...  15 us
  transfers between devices with their start and end apart: 31, of which 23 were waited for; matrix products, arithmetic and copies ran while one was open for 16% of the time, Pallas kernels for 4%

commit v1 on v0

--- a/solution.py
+++ b/solution.py
@@ -165,14 +165,25 @@
         + noise_rate * own_noise.astype(jnp.float32)
     ).astype(jnp.bfloat16)
 
-    def exchanged(blocks):
+    def exchanged(blocks, in_order):
         found = []
         for d in range(planes):
             to = lax.rem(plane + planes - d, planes)
             block = lax.dynamic_index_in_dim(blocks, to, 1, False)
             found.append(shifted_by(block, "fsdp", d, 1, planes) if d else block)
-        found = turned(jnp.stack(found), 0, planes - plane)
+        found = jnp.stack(found)
+        if in_order:
+            found = turned(found, 0, planes - plane)
         return found.reshape(planes, piece, rows)
+
+    def lined_up(value):
+        right, left = [value], [value]
+        for _ in range(planes - 1):
+            right.append(lax.ppermute(right[-1], "fsdp", [(p, p + 1) for p in range(planes - 1)]))
+            left.append(lax.ppermute(left[-1], "fsdp", [(p + 1, p) for p in range(planes - 1)]))
+        return [value] + [
+            jnp.where(plane + d < planes, left[d], right[planes - d]) for d in range(1, planes)
+        ]
 
     def gathered(clips):
         found = clips[: planes // 2], clips[planes // 2 :]
@@ -180,7 +191,7 @@
             found = gather_step(step, found, sides, chips, cores)
         return found
 
-    tokens = jnp.concatenate(gathered(exchanged(noised.reshape(piece, planes, rows))))
+    tokens = jnp.concatenate(gathered(exchanged(noised.reshape(piece, planes, rows), True)))
 
     sums = []
     for j in range(pairs):
@@ -191,7 +202,14 @@
 
     tokens, noised = lax.optimization_barrier((tokens, noised))
     columns = noised.reshape(piece, sides, planes, shard_rows).swapaxes(1, 2)
-    columns = jnp.concatenate(gathered(exchanged(columns)))
+    columns = jnp.concatenate(gathered(exchanged(columns, False)))
+
+    def settled(summed, j, own_grad, other):
+        other = other.astype(jnp.float32)
+        first = jnp.where(first_side, own_grad, other)
+        second = jnp.where(first_side, other, own_grad)
+        both = jnp.concatenate([first, second], axis=2)[:, :, : (heads - 2 * j) * HEAD]
+        return lax.dynamic_update_slice(summed, both, (0, 0, 2 * j * HEAD))
 
     own_up = own_order(upstream[0], order)
     groups = own_order(group_index[0], order)
@@ -199,18 +217,32 @@
         jnp.broadcast_to(groups[None, None, :], (1, 8, length)),
         jnp.broadcast_to(groups[None, :, None], (1, length, HEAD)),
     )
-    directions, cots = [], []
+    summed = jnp.zeros((3, shard_rows, head_cols), jnp.float32)
+    directions, done = [], []
     for j in range(pairs):
-        even, odd = sums[j][:, :, :HEAD], sums[j][:, :, -HEAD:]
+        (even, odd), done = lax.optimization_barrier(
+            ((sums[j][:, :, :HEAD], sums[j][:, :, -HEAD:]), done)
+        )
         kept = jnp.where(first_side, even, odd)
         swapped = lax.ppermute(jnp.where(first_side, odd, even), "mesh", swap)
+        if done:
+            summed = settled(summed, j - 1, *done)
         kept_head = jnp.minimum(2 * j + side, heads - 1)
         grad_out = lax.dynamic_slice_in_dim(own_up, kept_head * HEAD, HEAD, 1)
         direction, cotangents = attention(
             side, sides, kept[:, None], swapped[:, None], grad_out[None], groups
         )
         directions.append(direction[0])
-        cots.append(lax.all_gather(cotangents[:, 0], "fsdp", axis=0))
+        grad = None
+        for clip, cot in enumerate(lined_up(cotangents[:, 0])):
+            block = columns[clip * length : (clip + 1) * length]
+            product = dots(block, cot, ((0,), (1,)))
+            grad = product if grad is None else grad + product
+        grad = jnp.swapaxes(grad, 0, 1).reshape(3, sides, shard_rows, HEAD)
+        own_grad = jnp.where(first_side, grad[:, 0], grad[:, 1])
+        sent = jnp.where(first_side, grad[:, 1], grad[:, 0]).astype(jnp.bfloat16)
+        done = [own_grad, lax.ppermute(sent, "mesh", swap)]
+    summed = settled(summed, pairs - 1, *done)
 
     local = jnp.concatenate(directions, axis=1)
     local = local.reshape(sides, chips, cores, -1, pairs * HEAD)
@@ -225,21 +257,6 @@
     local = jnp.transpose(local, (2, 1, 3, 0, 4)).reshape(-1, lanes, pairs * sides, HEAD)
     direction = local[:, :, :heads].reshape(1, -1, lanes * head_cols)
 
-    summed = jnp.zeros((3, shard_rows, head_cols), jnp.float32)
-    for j in range(pairs):
-        grad = None
-        for clip in range(planes):
-            block = columns[clip * length : (clip + 1) * length]
-            product = dots(block, cots[j][clip], ((0,), (1,)))
-            grad = product if grad is None else grad + product
-        grad = jnp.swapaxes(grad, 0, 1).reshape(3, sides, shard_rows, HEAD)
-        own_grad = jnp.where(first_side, grad[:, 0], grad[:, 1])
-        sent = jnp.where(first_side, grad[:, 1], grad[:, 0]).astype(jnp.bfloat16)
-        other = lax.ppermute(sent, "mesh", swap).astype(jnp.float32)
-        first = jnp.where(first_side, own_grad, other)
-        second = jnp.where(first_side, other, own_grad)
-        both = jnp.concatenate([first, second], axis=2)[:, :, : (heads - 2 * j) * HEAD]
-        summed = lax.dynamic_update_slice(summed, both, (0, 0, 2 * j * HEAD))
     return (direction, jnp.swapaxes(summed, 0, 1))
 
 

time: 431 us -> 428 us (level)
  waiting for transfers between devices: 268 us -> 194 us
  starting transfers between devices: 34.1 us -> 98.8 us
  other arithmetic: 19.4 us -> 36.2 us
  local copies, waits for them, and re-layouts: 32.7 us -> 25.4 us
    ppermute x3 -> x21, waiting for transfers between devices: 18.7 us -> 100 us  [the longest x9 39.4 us: lined_up(): lax.ppermute(left[-1], 'fsdp', [(p + 1, p) for p in range(planes - 1)])]
    reduce_scatter x3, waiting for transfers between devices: 81 us -> 2.94 us  [per_device(): lax.psum_scatter(part, 'fsdp', scatter_dimension=0, tiled=True)[0]]
    ppermute x3 -> x21, starting transfers between devices: 3.63 us -> 70.5 us  [the longest x9 55.4 us: lined_up(): lax.ppermute(right[-1], 'fsdp', [(p, p + 1) for p in range(planes - 1)])]
    all_gather x3 -> x0, waiting for transfers between devices: 60.8 us -> none  [per_device(): cots.append(lax.all_gather(cotangents[:, 0], 'fsdp', axis=0))]
    ppermute x19, waiting for transfers between devices: 83.9 us -> 70.3 us  [shifted_by(): return lax.ppermute(value, axis, pairs)]
    select_n x3 -> x5, other arithmetic: 0.49 us -> 10.2 us  [the longest x2 5.15 us: per_device(): own_grad = jnp.where(first_side, grad[:, 0], grad[:, 1])]
    unnamed x54 -> x47, local copies, waits for them, and re-layouts: 12.3 us -> 5.29 us
  transfers between devices with their start and end apart: 31 -> 46, of which waited for: 23 -> 29; matrix products, arithmetic and copies ran while one was open for 16% -> 17% of each run, Pallas kernels for 4% -> 2%
where the time goes in v1:
time: 428 us; the launch traced here: 420 us
  waiting for transfers between devices  194 us (45%)
  starting transfers between devices  98.8 us (23%)
  other arithmetic  36.2 us (8%)
  matrix products  35.5 us (8%)
  local copies, waits for them, and re-layouts  25.4 us (6%)
  between operations  15.7 us (4%)
  Pallas kernels  15 us (4%)
    ppermute x19, waiting for transfers between devices, shifted_by(): return lax.ppermute(value, axis, pairs)  70.3 us
    ppermute x9, starting transfers between devices, lined_up(): lax.ppermute(right[-1], 'fsdp', [(p, p + 1) for p in range(planes - 1)])  55.4 us
    ppermute x9, waiting for transfers between devices, lined_up(): lax.ppermute(left[-1], 'fsdp', [(p + 1, p) for p in range(planes - 1)])  39.4 us
    ppermute x9, waiting for transfers between devices, lined_up(): lax.ppermute(right[-1], 'fsdp', [(p, p + 1) for p in range(planes - 1)])  39.1 us
    dot_general x15, matrix products, dots(): lax.dot_general(left, right, (dims, ((), ())), preferred_element_type=jnp...  35.5 us
    ppermute x19, starting transfers between devices, shifted_by(): return lax.ppermute(value, axis, pairs)  25.9 us
    ppermute x3, waiting for transfers between devices, per_device(): done = [own_grad, lax.ppermute(sent, 'mesh', swap)]  21.6 us
    ppermute x3, waiting for transfers between devices, per_device(): swapped = lax.ppermute(jnp.where(first_side, odd, even), 'mesh', swap)  20.3 us
  transfers between devices with their start and end apart: 46, of which 29 were waited for; matrix products, arithmetic and copies ran while one was open for 17% of the time, Pallas kernels for 2%

profile of v1, /device:TPU:0, one launch (start us, length us, event | category | flops | bytes accessed | tf_op | source)
XLA Modules:
  0.0 420.4 jit_solution(7637366239325229056)
XLA Ops:
  11.3 5.1 %collective-permute-start = (bf16[64,1280]{1,0:T(8,128)(2,1)S(1)}, bf16[64,1280]{1,0:T(8,128)(2,1)S(1)}, u32[]{:S(2)}, u32[]{:S(2)}) collective-permute-start(bf16[64,1280]{1,0:T(8,128)(2,1)S(1)} %bitcast.339), channel_id=1, source_target_pairs={{1,0},{2,1},{3,2},{0,3},{5,4},{6,5},{7,6},{4,7},{9,8},{10,9},{11,1... | collective-permute-start | bytes 491528 | tf_op jit(solution)/shard_map/ppermute | solution.py:18
  17.6 3.4 collective-permute-done
  21.1 9.2 %collective-permute-done.1 = bf16[64,1280]{1,0:T(8,128)(2,1)S(1)} collective-permute-done((bf16[64,1280]{1,0:T(8,128)(2,1)S(1)}, bf16[64,1280]{1,0:T(8,128)(2,1)S(1)}, u32[]{:S(2)}, u32[]{:S(2)}) %collective-permute-start.1) | collective-permute-done | bytes 163872 | tf_op jit(solution)/shard_map/ppermute | solution.py:18
  33.6 6.1 %collective-permute-done.3 = bf16[2,64,1280]{2,1,0:T(8,128)(2,1)S(1)} collective-permute-done((bf16[2,64,1280]{2,1,0:T(8,128)(2,1)S(1)}, bf16[2,64,1280]{2,1,0:T(8,128)(2,1)S(1)}, u32[]{:S(2)}, u32[]{:S(2)}) %collective-permute-start.3) | collective-permute-done | bytes 327712 | tf_op jit(solution)/shard_map/ppermute | solution.py:18
  43.0 12.1 %collective-permute-done.4 = bf16[2,2,64,1280]{3,2,0,1:T(8,128)(2,1)S(1)} collective-permute-done((bf16[2,2,64,1280]{3,2,0,1:T(8,128)(2,1)S(1)}, bf16[2,2,64,1280]{3,2,0,1:T(8,128)(2,1)S(1)}, u32[]{:S(2)}, u32[]{:S(2)}) %collective-permute-start.4) | collective-permute-done | bytes 655392 | tf_op jit(solution)/shard_map/ppermute | solution.py:18
  57.0 4.9 %collective-permute-done.7 = bf16[2,2,2,2,64,1280]{5,4,1,3,2,0:T(8,128)(2,1)S(1)} collective-permute-done((bf16[2,2,2,2,64,1280]{5,4,1,3,2,0:T(8,128)(2,1)S(1)}, bf16[2,2,2,2,64,1280]{5,4,1,3,2,0:T(8,128)(2,1)S(1)}, u32[]{:S(2)}, u32[]{:S(2)}) %collective-permute-start.7) | collective-permute-done | bytes 2621472 | tf_op jit(solution)/shard_map/ppermute | solution.py:18
  62.9 9.5 %fusion.6 = bf16[2048,3,256]{2,0,1:T(8,128)(2,1)S(1)} fusion(bf16[1,1280,3,768]{3,1,2,0:T(8,128)(2,1)} %param.10, bf16[1024,1280]{1,0:T(8,128)(2,1)S(1)} %bitcast.312, bf16[1024,1280]{1,0:T(8,128)(2,1)S(1)} %bitcast.309), kind=kOutput, calls=%fused_computation.17 | convolution fusion | flops 4038590464 | bytes 10354688 | tf_op jit(solution)/shard_map/dot_general | solution.py:51
  74.6 6.6 %fusion.9 = bf16[2048,3,256]{2,0,1:T(8,128)(2,1)S(1)} fusion(bf16[1,1280,3,768]{3,1,2,0:T(8,128)(2,1)} %param.10, bf16[1024,1280]{1,0:T(8,128)(2,1)} %bitcast.313, bf16[1024,1280]{1,0:T(8,128)(2,1)S(1)} %bitcast.310), kind=kOutput, calls=%fused_computation.18 | convolution fusion | flops 4038590464 | bytes 10354688 | tf_op jit(solution)/shard_map/dot_general | solution.py:51
  83.7 2.2 dynamic-slice_reduce_fusion
  85.9 2.5 collective-permute-start.12
  88.5 4.1 collective-permute-start.9
  92.6 15.7 %collective-permute-done.12 = bf16[64,2,640]{2,0,1:T(8,128)(2,1)S(1)} collective-permute-done((bf16[64,2,640]{2,0,1:T(8,128)(2,1)S(1)}, bf16[64,2,640]{2,0,1:T(8,128)(2,1)S(1)}, u32[]{:S(2)}, u32[]{:S(2)}) %collective-permute-start.12) | collective-permute-done | bytes 163872 | tf_op jit(solution)/shard_map/ppermute | solution.py:18
  112.5 6.0 %collective-permute-done.14 = bf16[2,64,1280]{2,1,0:T(8,128)(2,1)S(1)} collective-permute-done((bf16[2,64,1280]{2,1,0:T(8,128)(2,1)S(1)}, bf16[2,64,1280]{2,1,0:T(8,128)(2,1)S(1)}, u32[]{:S(2)}, u32[]{:S(2)}) %collective-permute-start.14) | collective-permute-done | bytes 327712 | tf_op jit(solution)/shard_map/ppermute | solution.py:18
  125.3 10.2 %collective-permute-done.15 = bf16[2,2,64,1280]{3,2,0,1:T(8,128)(2,1)} collective-permute-done((bf16[2,2,64,1280]{3,2,0,1:T(8,128)(2,1)}, bf16[2,2,64,1280]{3,2,0,1:T(8,128)(2,1)}, u32[]{:S(2)}, u32[]{:S(2)}) %collective-permute-start.15) | collective-permute-done | bytes 655392 | tf_op jit(solution)/shard_map/ppermute | solution.py:18
  139.4 2.0 pad_maximum_fusion.3
  141.4 2.9 reduce-scatter.4.cloned.1.call-done
  149.4 8.1 %collective-permute-done.8 = bf16[3,512,128]{2,1,0:T(8,128)(2,1)} collective-permute-done((bf16[3,512,128]{2,1,0:T(8,128)(2,1)}, bf16[3,512,128]{2,1,0:T(8,128)(2,1)}, u32[]{:S(2)}, u32[]{:S(2)}) %collective-permute-start.8) | collective-permute-done | bytes 393248 | tf_op jit(solution)/shard_map/ppermute | solution.py:227
  158.9 5.0 %attention.3 = (bf16[1,512,128]{2,1,0:T(8,128)(2,1)}, bf16[3,1,512,128]{3,2,1,0:T(8,128)(2,1)}) custom-call(s32[1]{0:T(128)} %bitcast.refs_0_, bf16[3,1,512,128]{3,2,1,0:T(8,128)(2,1)} %get-tuple-element.62.refs_1_, bf16[3,1,512,128]{3,2,1,0:T(8,128)(2,1)} %bitcast.28.refs_2_, bf16[1,512,128]{2,1,0:T(8,128)(2,1)} %get-tuple-element.56.refs_3_, ...), custom_call_target="tpu_custom_call" | custom-call | flops 603979776 | bytes 1310720 | tf_op jit(solution)/shard_map/attention/pallas_call | solution.py:116
  163.9 9.5 %collective-permute-start.18 = (bf16[3,512,128]{2,1,0:T(8,128)(2,1)}, bf16[3,512,128]{2,1,0:T(8,128)(2,1)S(1)}, u32[]{:S(2)}, u32[]{:S(2)}) collective-permute-start(bf16[3,512,128]{2,1,0:T(8,128)(2,1)} %bitcast.348), channel_id=1, source_target_pairs={{0,1},{1,2},{2,3},{4,5},{5,6},{6,7},{8,9},{9,10},{10,11},{12,13},{... | collective-permute-start | bytes 1179656 | tf_op jit(solution)/shard_map/ppermute | solution.py:182
  174.6 16.6 %collective-permute-done.18 = bf16[3,512,128]{2,1,0:T(8,128)(2,1)S(1)} collective-permute-done((bf16[3,512,128]{2,1,0:T(8,128)(2,1)}, bf16[3,512,128]{2,1,0:T(8,128)(2,1)S(1)}, u32[]{:S(2)}, u32[]{:S(2)}) %collective-permute-start.18) | collective-permute-done | bytes 393248 | tf_op jit(solution)/shard_map/ppermute | solution.py:182
  191.2 14.7 %collective-permute-start.19 = (bf16[3,512,128]{2,1,0:T(8,128)(2,1)S(1)}, bf16[3,512,128]{2,1,0:T(8,128)(2,1)}, u32[]{:S(2)}, u32[]{:S(2)}) collective-permute-start(bf16[3,512,128]{2,1,0:T(8,128)(2,1)S(1)} %collective-permute-done.18), channel_id=1, source_target_pairs={{0,1},{1,2},{2,3},{4,5},{5,6},{6,7},{8,9},{9,10},{10,11},{12,13},{... | collective-permute-start | bytes 1179656 | tf_op jit(solution)/shard_map/ppermute | solution.py:182
  205.9 7.4 %fusion.12 = bf16[2048,3,256]{2,0,1:T(8,128)(2,1)S(1)} fusion(bf16[1,1280,3,768]{3,1,2,0:T(8,128)(2,1)} %param.10, bf16[1024,1280]{1,0:T(8,128)(2,1)} %bitcast.314, bf16[1024,1280]{1,0:T(8,128)(2,1)} %bitcast.311), kind=kOutput, calls=%fused_computation.19 | convolution fusion | flops 4038590464 | bytes 10354688 | tf_op jit(solution)/shard_map/dot_general | solution.py:51
  216.5 5.6 %collective-permute-done.19 = bf16[3,512,128]{2,1,0:T(8,128)(2,1)} collective-permute-done((bf16[3,512,128]{2,1,0:T(8,128)(2,1)S(1)}, bf16[3,512,128]{2,1,0:T(8,128)(2,1)}, u32[]{:S(2)}, u32[]{:S(2)}) %collective-permute-start.19) | collective-permute-done | bytes 393248 | tf_op jit(solution)/shard_map/ppermute | solution.py:182
  222.1 5.0 %collective-permute-start.20 = (bf16[3,512,128]{2,1,0:T(8,128)(2,1)}, bf16[3,512,128]{2,1,0:T(8,128)(2,1)S(1)}, u32[]{:S(2)}, u32[]{:S(2)}) collective-permute-start(bf16[3,512,128]{2,1,0:T(8,128)(2,1)} %collective-permute-done.19), channel_id=1, source_target_pairs={{0,1},{1,2},{2,3},{4,5},{5,6},{6,7},{8,9},{9,10},{10,11},{12,13},{... | collective-permute-start | bytes 1179656 | tf_op jit(solution)/shard_map/ppermute | solution.py:182
  234.7 23.3 %collective-permute-done.22 = bf16[3,512,128]{2,1,0:T(8,128)(2,1)S(1)} collective-permute-done((bf16[3,512,128]{2,1,0:T(8,128)(2,1)S(1)}, bf16[3,512,128]{2,1,0:T(8,128)(2,1)S(1)}, u32[]{:S(2)}, u32[]{:S(2)}) %collective-permute-start.22) | collective-permute-done | bytes 393248 | tf_op jit(solution)/shard_map/ppermute | solution.py:183
  262.3 2.6 select_bitcast_fusion.1
  264.9 9.5 %collective-permute-done.23 = bf16[3,640,128]{2,1,0:T(8,128)(2,1)S(1)} collective-permute-done((bf16[3,640,128]{2,1,0:T(8,128)(2,1)}, bf16[3,640,128]{2,1,0:T(8,128)(2,1)S(1)}, u32[]{:S(2)}, u32[]{:S(2)}) %collective-permute-start.23) | collective-permute-done | bytes 491552 | tf_op jit(solution)/shard_map/ppermute | solution.py:244
  275.2 7.8 %collective-permute-done.24 = bf16[3,512,128]{2,1,0:T(8,128)(2,1)S(1)} collective-permute-done((bf16[3,512,128]{2,1,0:T(8,128)(2,1)S(1)}, bf16[3,512,128]{2,1,0:T(8,128)(2,1)S(1)}, u32[]{:S(2)}, u32[]{:S(2)}) %collective-permute-start.24) | collective-permute-done | bytes 393248 | tf_op jit(solution)/shard_map/ppermute | solution.py:227
  283.7 5.0 %attention.4 = (bf16[1,512,128]{2,1,0:T(8,128)(2,1)}, bf16[3,1,512,128]{3,2,1,0:T(8,128)(2,1)}) custom-call(s32[1]{0:T(128)} %bitcast.refs_0_, bf16[3,1,512,128]{3,2,1,0:T(8,128)(2,1)} %get-tuple-element.60.refs_1_, bf16[3,1,512,128]{3,2,1,0:T(8,128)(2,1)} %bitcast.354, bf16[1,512,128]{2,1,0:T(8,128)(2,1)} %get-tuple-element.55.refs_3_, ...), custom_call_target="tpu_custom_call" | custom-call | flops 603979776 | bytes 1310720 | tf_op jit(solution)/shard_map/attention/pallas_call | solution.py:116
  288.7 6.3 %collective-permute-start.26 = (bf16[3,512,128]{2,1,0:T(8,128)(2,1)}, bf16[3,512,128]{2,1,0:T(8,128)(2,1)S(1)}, u32[]{:S(2)}, u32[]{:S(2)}) collective-permute-start(bf16[3,512,128]{2,1,0:T(8,128)(2,1)} %bitcast.352), channel_id=1, source_target_pairs={{0,1},{1,2},{2,3},{4,5},{5,6},{6,7},{8,9},{9,10},{10,11},{12,13},{... | collective-permute-start | bytes 1179656 | tf_op jit(solution)/shard_map/ppermute | solution.py:182
  296.3 7.5 %collective-permute-done.26 = bf16[3,512,128]{2,1,0:T(8,128)(2,1)S(1)} collective-permute-done((bf16[3,512,128]{2,1,0:T(8,128)(2,1)}, bf16[3,512,128]{2,1,0:T(8,128)(2,1)S(1)}, u32[]{:S(2)}, u32[]{:S(2)}) %collective-permute-start.26) | collective-permute-done | bytes 393248 | tf_op jit(solution)/shard_map/ppermute | solution.py:182
  303.9 4.3 %collective-permute-start.27 = (bf16[3,512,128]{2,1,0:T(8,128)(2,1)S(1)}, bf16[3,512,128]{2,1,0:T(8,128)(2,1)S(1)}, u32[]{:S(2)}, u32[]{:S(2)}) collective-permute-start(bf16[3,512,128]{2,1,0:T(8,128)(2,1)S(1)} %collective-permute-done.26), channel_id=1, source_target_pairs={{0,1},{1,2},{2,3},{4,5},{5,6},{6,7},{8,9},{9,10},{10,11},{12,13},{... | collective-permute-start | bytes 1179656 | tf_op jit(solution)/shard_map/ppermute | solution.py:182
  309.5 6.4 %collective-permute-done.27 = bf16[3,512,128]{2,1,0:T(8,128)(2,1)S(1)} collective-permute-done((bf16[3,512,128]{2,1,0:T(8,128)(2,1)S(1)}, bf16[3,512,128]{2,1,0:T(8,128)(2,1)S(1)}, u32[]{:S(2)}, u32[]{:S(2)}) %collective-permute-start.27) | collective-permute-done | bytes 393248 | tf_op jit(solution)/shard_map/ppermute | solution.py:182
  315.8 4.4 %collective-permute-start.28 = (bf16[3,512,128]{2,1,0:T(8,128)(2,1)S(1)}, bf16[3,512,128]{2,1,0:T(8,128)(2,1)S(1)}, u32[]{:S(2)}, u32[]{:S(2)}) collective-permute-start(bf16[3,512,128]{2,1,0:T(8,128)(2,1)S(1)} %collective-permute-done.27), channel_id=1, source_target_pairs={{0,1},{1,2},{2,3},{4,5},{5,6},{6,7},{8,9},{9,10},{10,11},{12,13},{... | collective-permute-start | bytes 1179656 | tf_op jit(solution)/shard_map/ppermute | solution.py:182
  320.2 2.3 fusion.64
  327.3 4.9 %collective-permute-done.30 = bf16[3,512,128]{2,1,0:T(8,128)(2,1)S(1)} collective-permute-done((bf16[3,512,128]{2,1,0:T(8,128)(2,1)S(1)}, bf16[3,512,128]{2,1,0:T(8,128)(2,1)S(1)}, u32[]{:S(2)}, u32[]{:S(2)}) %collective-permute-start.30) | collective-permute-done | bytes 393248 | tf_op jit(solution)/shard_map/ppermute | solution.py:183
  337.8 2.6 select_bitcast_fusion
  340.4 5.6 %collective-permute-done.31 = bf16[3,640,128]{2,1,0:T(8,128)(2,1)} collective-permute-done((bf16[3,640,128]{2,1,0:T(8,128)(2,1)}, bf16[3,640,128]{2,1,0:T(8,128)(2,1)}, u32[]{:S(2)}, u32[]{:S(2)}) %collective-permute-start.31) | collective-permute-done | bytes 491552 | tf_op jit(solution)/shard_map/ppermute | solution.py:244
  347.5 2.7 convert_select_fusion.5
  350.2 4.5 %collective-permute-done.32 = bf16[3,512,128]{2,1,0:T(8,128)(2,1)} collective-permute-done((bf16[3,512,128]{2,1,0:T(8,128)(2,1)S(1)}, bf16[3,512,128]{2,1,0:T(8,128)(2,1)}, u32[]{:S(2)}, u32[]{:S(2)}) %collective-permute-start.32) | collective-permute-done | bytes 393248 | tf_op jit(solution)/shard_map/ppermute | solution.py:227
  354.7 5.0 %attention.5 = (bf16[1,512,128]{2,1,0:T(8,128)(2,1)}, bf16[3,1,512,128]{3,2,1,0:T(8,128)(2,1)}) custom-call(s32[1]{0:T(128)} %bitcast.refs_0_, bf16[3,1,512,128]{3,2,1,0:T(8,128)(2,1)} %get-tuple-element.58.refs_1_, bf16[3,1,512,128]{3,2,1,0:T(8,128)(2,1)} %bitcast.91.refs_2_, bf16[1,512,128]{2,1,0:T(8,128)(2,1)} %get-tuple-element.54.refs_3_, ...), custom_call_target="tpu_custom_call" | custom-call | flops 603979776 | bytes 1310720 | tf_op jit(solution)/shard_map/attention/pallas_call | solution.py:116
  359.7 2.3 collective-permute-start.37
  362.0 4.6 %select_maximum_fusion = f32[3,640,768]{2,1,0:T(8,128)} fusion(f32[3,640,128]{2,1,0:T(8,128)} %get-tuple-element.51, f32[3,640,128]{2,1,0:T(8,128)} %get-tuple-element.50), kind=kLoop, calls=%fused_computation.6 | loop fusion | flops 5898240 | bytes 7864320 | tf_op jit(solution)/shard_map/concatenate | solution.py:211
  368.7 4.6 %collective-permute-start.38 = (bf16[3,512,128]{2,1,0:T(8,128)(2,1)S(1)}, bf16[3,512,128]{2,1,0:T(8,128)(2,1)S(1)}, u32[]{:S(2)}, u32[]{:S(2)}) collective-permute-start(bf16[3,512,128]{2,1,0:T(8,128)(2,1)S(1)} %collective-permute-done.37), channel_id=1, source_target_pairs={{0,1},{1,2},{2,3},{4,5},{5,6},{6,7},{8,9},{9,10},{10,11},{12,13},{... | collective-permute-start | bytes 1179656 | tf_op jit(solution)/shard_map/ppermute | solution.py:182
  378.5 4.4 %collective-permute-start.39 = (bf16[3,512,128]{2,1,0:T(8,128)(2,1)S(1)}, bf16[3,512,128]{2,1,0:T(8,128)(2,1)S(1)}, u32[]{:S(2)}, u32[]{:S(2)}) collective-permute-start(bf16[3,512,128]{2,1,0:T(8,128)(2,1)S(1)} %collective-permute-done.38), channel_id=1, source_target_pairs={{0,1},{1,2},{2,3},{4,5},{5,6},{6,7},{8,9},{9,10},{10,11},{12,13},{... | collective-permute-start | bytes 1179656 | tf_op jit(solution)/shard_map/ppermute | solution.py:182
  384.0 2.1 collective-permute-done.40
  390.0 7.4 %collective-permute-done.41 = bf16[3,512,128]{2,1,0:T(8,128)(2,1)S(1)} collective-permute-done((bf16[3,512,128]{2,1,0:T(8,128)(2,1)S(1)}, bf16[3,512,128]{2,1,0:T(8,128)(2,1)S(1)}, u32[]{:S(2)}, u32[]{:S(2)}) %collective-permute-start.41) | collective-permute-done | bytes 393248 | tf_op jit(solution)/shard_map/ppermute | solution.py:183
  404.5 6.5 %collective-permute-done.42 = bf16[3,640,128]{2,1,0:T(8,128)(2,1)} collective-permute-done((bf16[3,640,128]{2,1,0:T(8,128)(2,1)}, bf16[3,640,128]{2,1,0:T(8,128)(2,1)}, u32[]{:S(2)}, u32[]{:S(2)}) %collective-permute-start.42) | collective-permute-done | bytes 491552 | tf_op jit(solution)/shard_map/ppermute | solution.py:244
  (196 shorter events, 94.0 us)
Async XLA Ops:
  7.2 137.2 %reduce-scatter.4.cloned.1.call-start = ((), (), s32[]{:S(2)}) async-start(), calls=%async_computation.3 | async-start | bytes 3932160 | tf_op jit(solution)/shard_map/reduce_scatter | solution.py:201
  11.3 9.8 %collective-permute-start = (bf16[64,1280]{1,0:T(8,128)(2,1)S(1)}, bf16[64,1280]{1,0:T(8,128)(2,1)S(1)}, u32[]{:S(2)}, u32[]{:S(2)}) collective-permute-start(bf16[64,1280]{1,0:T(8,128)(2,1)S(1)} %bitcast.339), channel_id=1, source_target_pairs={{1,0},{2,1},{3,2},{0,3},{5,4},{6,5},{7,6},{4,7},{9,8},{10,9},{11,1... | collective-permute-start | bytes 491528 | tf_op jit(solution)/shard_map/ppermute | solution.py:18
  16.4 13.9 %collective-permute-start.1 = (bf16[64,1280]{1,0:T(8,128)(2,1)S(1)}, bf16[64,1280]{1,0:T(8,128)(2,1)S(1)}, u32[]{:S(2)}, u32[]{:S(2)}) collective-permute-start(bf16[64,1280]{1,0:T(8,128)(2,1)S(1)} %bitcast.340), channel_id=1, source_target_pairs={{2,0},{3,1},{0,2},{1,3},{6,4},{7,5},{4,6},{5,7},{10,8},{11,9},{8,1... | collective-permute-start | bytes 491528 | tf_op jit(solution)/shard_map/ppermute | solution.py:18
  16.5 13.8 %collective-permute-start.2 = (bf16[64,1280]{1,0:T(8,128)(2,1)S(1)}, bf16[64,1280]{1,0:T(8,128)(2,1)S(1)}, u32[]{:S(2)}, u32[]{:S(2)}) collective-permute-start(bf16[64,1280]{1,0:T(8,128)(2,1)S(1)} %bitcast.341), channel_id=1, source_target_pairs={{3,0},{0,1},{1,2},{2,3},{7,4},{4,5},{5,6},{6,7},{11,8},{8,9},{9,10... | collective-permute-start | bytes 491528 | tf_op jit(solution)/shard_map/ppermute | solution.py:18
  30.5 9.2 %collective-permute-start.3 = (bf16[2,64,1280]{2,1,0:T(8,128)(2,1)S(1)}, bf16[2,64,1280]{2,1,0:T(8,128)(2,1)S(1)}, u32[]{:S(2)}, u32[]{:S(2)}) collective-permute-start(bf16[2,64,1280]{2,1,0:T(8,128)(2,1)S(1)} %get-tuple-element.52), channel_id=1, source_target_pairs={{16,0},{0,16},{17,1},{1,17},{18,2},{2,18},{19,3},{3,19},{20,4},{4,... | collective-permute-start | bytes 983048 | tf_op jit(solution)/shard_map/ppermute | solution.py:18
  32.1 9.3 %collective-permute-start.5 = (bf16[2,64,1280]{2,1,0:T(8,128)(2,1)S(1)}, bf16[2,64,1280]{2,1,0:T(8,128)(2,1)S(1)}, u32[]{:S(2)}, u32[]{:S(2)}) collective-permute-start(bf16[2,64,1280]{2,1,0:T(8,128)(2,1)S(1)} %get-tuple-element.53), channel_id=1, source_target_pairs={{8,0},{12,4},{0,8},{4,12},{9,1},{13,5},{1,9},{5,13},{10,2},{14,6},... | collective-permute-start | bytes 983048 | tf_op jit(solution)/shard_map/ppermute | solution.py:18
  39.8 15.3 %collective-permute-start.4 = (bf16[2,2,64,1280]{3,2,0,1:T(8,128)(2,1)S(1)}, bf16[2,2,64,1280]{3,2,0,1:T(8,128)(2,1)S(1)}, u32[]{:S(2)}, u32[]{:S(2)}) collective-permute-start(bf16[2,2,64,1280]{3,2,0,1:T(8,128)(2,1)S(1)} %get-tuple-element.78), channel_id=1, source_target_pairs={{8,0},{12,4},{0,8},{4,12},{9,1},{13,5},{1,9},{5,13},{10,2},{14,6},... | collective-permute-start | bytes 1966088 | tf_op jit(solution)/shard_map/ppermute | solution.py:18
  41.4 15.0 %collective-permute-start.6 = (bf16[2,2,64,1280]{3,2,0,1:T(8,128)(2,1)S(1)}, bf16[2,2,64,1280]{3,2,0,1:T(8,128)(2,1)S(1)}, u32[]{:S(2)}, u32[]{:S(2)}) collective-permute-start(bf16[2,2,64,1280]{3,2,0,1:T(8,128)(2,1)S(1)} %get-tuple-element.80), channel_id=1, source_target_pairs={{16,0},{0,16},{17,1},{1,17},{18,2},{2,18},{19,3},{3,19},{20,4},{4,... | collective-permute-start | bytes 1966088 | tf_op jit(solution)/shard_map/ppermute | solution.py:18
  56.9 5.0 %collective-permute-start.7 = (bf16[2,2,2,2,64,1280]{5,4,1,3,2,0:T(8,128)(2,1)S(1)}, bf16[2,2,2,2,64,1280]{5,4,1,3,2,0:T(8,128)(2,1)S(1)}, u32[]{:S(2)}, u32[]{:S(2)}) collective-permute-start(bf16[2,2,2,2,64,1280]{5,4,1,3,2,0:T(8,128)(2,1)S(1)} %get-tuple-element.45), channel_id=1, source_target_pairs={{4,0},{0,4},{12,8},{8,12},{5,1},{1,5},{13,9},{9,13},{6,2},{2,6},{1... | collective-permute-start | bytes 7864328 | tf_op jit(solution)/shard_map/ppermute | solution.py:18
  74.3 186.8 %reduce-scatter.6.cloned.1.call-start = ((), (), s32[]{:S(2)}) async-start(), calls=%async_computation.4 | async-start | bytes 3932160 | tf_op jit(solution)/shard_map/reduce_scatter | solution.py:201
  83.1 253.5 %reduce-scatter.8.cloned.1.call-start = ((), (), s32[]{:S(2)}) async-start(), calls=%async_computation.5 | async-start | bytes 3932160 | tf_op jit(solution)/shard_map/reduce_scatter | solution.py:201
  85.9 22.4 %collective-permute-start.12 = (bf16[64,2,640]{2,0,1:T(8,128)(2,1)S(1)}, bf16[64,2,640]{2,0,1:T(8,128)(2,1)S(1)}, u32[]{:S(2)}, u32[]{:S(2)}) collective-permute-start(bf16[64,2,640]{2,0,1:T(8,128)(2,1)S(1)} %bitcast.344), channel_id=1, source_target_pairs={{2,0},{3,1},{0,2},{1,3},{6,4},{7,5},{4,6},{5,7},{10,8},{11,9},{8,1... | collective-permute-start | bytes 491528 | tf_op jit(solution)/shard_map/ppermute | solution.py:18
  88.4 20.2 %collective-permute-start.13 = (bf16[64,2,640]{2,0,1:T(8,128)(2,1)S(1)}, bf16[64,2,640]{2,0,1:T(8,128)(2,1)S(1)}, u32[]{:S(2)}, u32[]{:S(2)}) collective-permute-start(bf16[64,2,640]{2,0,1:T(8,128)(2,1)S(1)} %bitcast.343), channel_id=1, source_target_pairs={{3,0},{0,1},{1,2},{2,3},{7,4},{4,5},{5,6},{6,7},{11,8},{8,9},{9,10... | collective-permute-start | bytes 491528 | tf_op jit(solution)/shard_map/ppermute | solution.py:18
  88.5 21.9 %collective-permute-start.9 = (bf16[64,2,640]{2,0,1:T(8,128)(2,1)S(1)}, bf16[64,2,640]{2,0,1:T(8,128)(2,1)S(1)}, u32[]{:S(2)}, u32[]{:S(2)}) collective-permute-start(bf16[64,2,640]{2,0,1:T(8,128)(2,1)S(1)} %bitcast.342), channel_id=1, source_target_pairs={{1,0},{2,1},{3,2},{0,3},{5,4},{6,5},{7,6},{4,7},{9,8},{10,9},{11,1... | collective-permute-start | bytes 491528 | tf_op jit(solution)/shard_map/ppermute | solution.py:18
  108.9 9.6 %collective-permute-start.14 = (bf16[2,64,1280]{2,1,0:T(8,128)(2,1)S(1)}, bf16[2,64,1280]{2,1,0:T(8,128)(2,1)S(1)}, u32[]{:S(2)}, u32[]{:S(2)}) collective-permute-start(bf16[2,64,1280]{2,1,0:T(8,128)(2,1)S(1)} %pad_maximum_fusion.11), channel_id=1, source_target_pairs={{8,0},{12,4},{0,8},{4,12},{9,1},{13,5},{1,9},{5,13},{10,2},{14,6},... | collective-permute-start | bytes 983048 | tf_op jit(solution)/shard_map/ppermute | solution.py:18
  110.8 10.4 %collective-permute-start.10 = (bf16[2,64,1280]{2,1,0:T(8,128)(2,1)S(1)}, bf16[2,64,1280]{2,1,0:T(8,128)(2,1)S(1)}, u32[]{:S(2)}, u32[]{:S(2)}) collective-permute-start(bf16[2,64,1280]{2,1,0:T(8,128)(2,1)S(1)} %pad_maximum_fusion.10), channel_id=1, source_target_pairs={{16,0},{0,16},{17,1},{1,17},{18,2},{2,18},{19,3},{3,19},{20,4},{4,... | collective-permute-start | bytes 983048 | tf_op jit(solution)/shard_map/ppermute | solution.py:18
  119.4 16.1 %collective-permute-start.15 = (bf16[2,2,64,1280]{3,2,0,1:T(8,128)(2,1)}, bf16[2,2,64,1280]{3,2,0,1:T(8,128)(2,1)}, u32[]{:S(2)}, u32[]{:S(2)}) collective-permute-start(bf16[2,2,64,1280]{3,2,0,1:T(8,128)(2,1)} %get-tuple-element.76), channel_id=1, source_target_pairs={{16,0},{0,16},{17,1},{1,17},{18,2},{2,18},{19,3},{3,19},{20,4},{4,... | collective-permute-start | bytes 1966088 | tf_op jit(solution)/shard_map/ppermute | solution.py:18
  122.1 16.1 %collective-permute-start.11 = (bf16[2,2,64,1280]{3,2,1,0:T(8,128)(2,1)}, bf16[2,2,64,1280]{3,2,1,0:T(8,128)(2,1)}, u32[]{:S(2)}, u32[]{:S(2)}) collective-permute-start(bf16[2,2,64,1280]{3,2,1,0:T(8,128)(2,1)} %get-tuple-element.70), channel_id=1, source_target_pairs={{8,0},{12,4},{0,8},{4,12},{9,1},{13,5},{1,9},{5,13},{10,2},{14,6},... | collective-permute-start | bytes 1966088 | tf_op jit(solution)/shard_map/ppermute | solution.py:18
  141.3 85.8 %collective-permute-start.16 = (bf16[2,2,2,2,64,1280]{5,4,2,1,3,0:T(8,128)(2,1)}, bf16[2,2,2,2,64,1280]{5,4,2,1,3,0:T(8,128)(2,1)}, u32[]{:S(2)}, u32[]{:S(2)}) collective-permute-start(bf16[2,2,2,2,64,1280]{5,4,2,1,3,0:T(8,128)(2,1)} %get-tuple-element.42), channel_id=1, source_target_pairs={{4,0},{0,4},{12,8},{8,12},{5,1},{1,5},{13,9},{9,13},{6,2},{2,6},{1... | collective-permute-start | bytes 7864328 | tf_op jit(solution)/shard_map/ppermute | solution.py:18
  146.4 11.0 %collective-permute-start.8 = (bf16[3,512,128]{2,1,0:T(8,128)(2,1)}, bf16[3,512,128]{2,1,0:T(8,128)(2,1)}, u32[]{:S(2)}, u32[]{:S(2)}) collective-permute-start(bf16[3,512,128]{2,1,0:T(8,128)(2,1)} %get-tuple-element.61), channel_id=1, source_target_pairs={{0,16},{16,0},{1,17},{17,1},{2,18},{18,2},{3,19},{19,3},{4,20},{20... | collective-permute-start | bytes 1179656 | tf_op jit(solution)/shard_map/ppermute | solution.py:227
  163.9 27.4 %collective-permute-start.18 = (bf16[3,512,128]{2,1,0:T(8,128)(2,1)}, bf16[3,512,128]{2,1,0:T(8,128)(2,1)S(1)}, u32[]{:S(2)}, u32[]{:S(2)}) collective-permute-start(bf16[3,512,128]{2,1,0:T(8,128)(2,1)} %bitcast.348), channel_id=1, source_target_pairs={{0,1},{1,2},{2,3},{4,5},{5,6},{6,7},{8,9},{9,10},{10,11},{12,13},{... | collective-permute-start | bytes 1179656 | tf_op jit(solution)/shard_map/ppermute | solution.py:182
  173.3 41.9 %collective-permute-start.17 = (bf16[3,512,128]{2,1,0:T(8,128)(2,1)}, bf16[3,512,128]{2,1,0:T(8,128)(2,1)S(1)}, u32[]{:S(2)}, u32[]{:S(2)}) collective-permute-start(bf16[3,512,128]{2,1,0:T(8,128)(2,1)} %bitcast.349), channel_id=1, source_target_pairs={{1,0},{2,1},{3,2},{5,4},{6,5},{7,6},{9,8},{10,9},{11,10},{13,12},{... | collective-permute-start | bytes 1179656 | tf_op jit(solution)/shard_map/ppermute | solution.py:183
  191.2 30.9 %collective-permute-start.19 = (bf16[3,512,128]{2,1,0:T(8,128)(2,1)S(1)}, bf16[3,512,128]{2,1,0:T(8,128)(2,1)}, u32[]{:S(2)}, u32[]{:S(2)}) collective-permute-start(bf16[3,512,128]{2,1,0:T(8,128)(2,1)S(1)} %collective-permute-done.18), channel_id=1, source_target_pairs={{0,1},{1,2},{2,3},{4,5},{5,6},{6,7},{8,9},{9,10},{10,11},{12,13},{... | collective-permute-start | bytes 1179656 | tf_op jit(solution)/shard_map/ppermute | solution.py:182
  215.2 16.3 %collective-permute-start.21 = (bf16[3,512,128]{2,1,0:T(8,128)(2,1)S(1)}, bf16[3,512,128]{2,1,0:T(8,128)(2,1)S(1)}, u32[]{:S(2)}, u32[]{:S(2)}) collective-permute-start(bf16[3,512,128]{2,1,0:T(8,128)(2,1)S(1)} %collective-permute-done.17), channel_id=1, source_target_pairs={{1,0},{2,1},{3,2},{5,4},{6,5},{7,6},{9,8},{10,9},{11,10},{13,12},{... | collective-permute-start | bytes 1179656 | tf_op jit(solution)/shard_map/ppermute | solution.py:183
  222.1 10.7 %collective-permute-start.20 = (bf16[3,512,128]{2,1,0:T(8,128)(2,1)}, bf16[3,512,128]{2,1,0:T(8,128)(2,1)S(1)}, u32[]{:S(2)}, u32[]{:S(2)}) collective-permute-start(bf16[3,512,128]{2,1,0:T(8,128)(2,1)} %collective-permute-done.19), channel_id=1, source_target_pairs={{0,1},{1,2},{2,3},{4,5},{5,6},{6,7},{8,9},{9,10},{10,11},{12,13},{... | collective-permute-start | bytes 1179656 | tf_op jit(solution)/shard_map/ppermute | solution.py:182
  231.6 26.4 %collective-permute-start.22 = (bf16[3,512,128]{2,1,0:T(8,128)(2,1)S(1)}, bf16[3,512,128]{2,1,0:T(8,128)(2,1)S(1)}, u32[]{:S(2)}, u32[]{:S(2)}) collective-permute-start(bf16[3,512,128]{2,1,0:T(8,128)(2,1)S(1)} %collective-permute-done.21), channel_id=1, source_target_pairs={{1,0},{2,1},{3,2},{5,4},{6,5},{7,6},{9,8},{10,9},{11,10},{13,12},{... | collective-permute-start | bytes 1179656 | tf_op jit(solution)/shard_map/ppermute | solution.py:183
  261.1 13.3 %collective-permute-start.23 = (bf16[3,640,128]{2,1,0:T(8,128)(2,1)}, bf16[3,640,128]{2,1,0:T(8,128)(2,1)S(1)}, u32[]{:S(2)}, u32[]{:S(2)}) collective-permute-start(bf16[3,640,128]{2,1,0:T(8,128)(2,1)} %fusion.29), channel_id=1, source_target_pairs={{0,16},{16,0},{1,17},{17,1},{2,18},{18,2},{3,19},{19,3},{4,20},{20... | collective-permute-start | bytes 1474568 | tf_op jit(solution)/shard_map/ppermute | solution.py:244
  275.2 7.8 %collective-permute-start.24 = (bf16[3,512,128]{2,1,0:T(8,128)(2,1)S(1)}, bf16[3,512,128]{2,1,0:T(8,128)(2,1)S(1)}, u32[]{:S(2)}, u32[]{:S(2)}) collective-permute-start(bf16[3,512,128]{2,1,0:T(8,128)(2,1)S(1)} %get-tuple-element.59), channel_id=1, source_target_pairs={{0,16},{16,0},{1,17},{17,1},{2,18},{18,2},{3,19},{19,3},{4,20},{20... | collective-permute-start | bytes 1179656 | tf_op jit(solution)/shard_map/ppermute | solution.py:227
  288.7 36.8 %copy-start.1 = (bf16[1,1,2,2,2,64,1280]{6,5,4,3,2,1,0:T(8,128)(2,1)S(1)}, bf16[1,1,2,2,2,64,1280]{6,5,4,3,2,1,0:T(8,128)(2,1)}, u32[]{:S(2)}) copy-start(bf16[1,1,2,2,2,64,1280]{6,5,4,3,2,1,0:T(8,128)(2,1)} %copy-done) | copy-start | bytes 3932164
  288.7 15.2 %collective-permute-start.26 = (bf16[3,512,128]{2,1,0:T(8,128)(2,1)}, bf16[3,512,128]{2,1,0:T(8,128)(2,1)S(1)}, u32[]{:S(2)}, u32[]{:S(2)}) collective-permute-start(bf16[3,512,128]{2,1,0:T(8,128)(2,1)} %bitcast.352), channel_id=1, source_target_pairs={{0,1},{1,2},{2,3},{4,5},{5,6},{6,7},{8,9},{9,10},{10,11},{12,13},{... | collective-permute-start | bytes 1179656 | tf_op jit(solution)/shard_map/ppermute | solution.py:182
  295.0 13.1 %collective-permute-start.25 = (bf16[3,512,128]{2,1,0:T(8,128)(2,1)}, bf16[3,512,128]{2,1,0:T(8,128)(2,1)S(1)}, u32[]{:S(2)}, u32[]{:S(2)}) collective-permute-start(bf16[3,512,128]{2,1,0:T(8,128)(2,1)} %bitcast.353), channel_id=1, source_target_pairs={{1,0},{2,1},{3,2},{5,4},{6,5},{7,6},{9,8},{10,9},{11,10},{13,12},{... | collective-permute-start | bytes 1179656 | tf_op jit(solution)/shard_map/ppermute | solution.py:183
  303.9 12.0 %collective-permute-start.27 = (bf16[3,512,128]{2,1,0:T(8,128)(2,1)S(1)}, bf16[3,512,128]{2,1,0:T(8,128)(2,1)S(1)}, u32[]{:S(2)}, u32[]{:S(2)}) collective-permute-start(bf16[3,512,128]{2,1,0:T(8,128)(2,1)S(1)} %collective-permute-done.26), channel_id=1, source_target_pairs={{0,1},{1,2},{2,3},{4,5},{5,6},{6,7},{8,9},{9,10},{10,11},{12,13},{... | collective-permute-start | bytes 1179656 | tf_op jit(solution)/shard_map/ppermute | solution.py:182
  308.2 14.3 %collective-permute-start.29 = (bf16[3,512,128]{2,1,0:T(8,128)(2,1)S(1)}, bf16[3,512,128]{2,1,0:T(8,128)(2,1)S(1)}, u32[]{:S(2)}, u32[]{:S(2)}) collective-permute-start(bf16[3,512,128]{2,1,0:T(8,128)(2,1)S(1)} %collective-permute-done.25), channel_id=1, source_target_pairs={{1,0},{2,1},{3,2},{5,4},{6,5},{7,6},{9,8},{10,9},{11,10},{13,12},{... | collective-permute-start | bytes 1179656 | tf_op jit(solution)/shard_map/ppermute | solution.py:183
  315.8 9.7 %collective-permute-start.28 = (bf16[3,512,128]{2,1,0:T(8,128)(2,1)S(1)}, bf16[3,512,128]{2,1,0:T(8,128)(2,1)S(1)}, u32[]{:S(2)}, u32[]{:S(2)}) collective-permute-start(bf16[3,512,128]{2,1,0:T(8,128)(2,1)S(1)} %collective-permute-done.27), channel_id=1, source_target_pairs={{0,1},{1,2},{2,3},{4,5},{5,6},{6,7},{8,9},{9,10},{10,11},{12,13},{... | collective-permute-start | bytes 1179656 | tf_op jit(solution)/shard_map/ppermute | solution.py:182
  322.5 9.7 %collective-permute-start.30 = (bf16[3,512,128]{2,1,0:T(8,128)(2,1)S(1)}, bf16[3,512,128]{2,1,0:T(8,128)(2,1)S(1)}, u32[]{:S(2)}, u32[]{:S(2)}) collective-permute-start(bf16[3,512,128]{2,1,0:T(8,128)(2,1)S(1)} %collective-permute-done.29), channel_id=1, source_target_pairs={{1,0},{2,1},{3,2},{5,4},{6,5},{7,6},{9,8},{10,9},{11,10},{13,12},{... | collective-permute-start | bytes 1179656 | tf_op jit(solution)/shard_map/ppermute | solution.py:183
  335.3 10.8 %collective-permute-start.31 = (bf16[3,640,128]{2,1,0:T(8,128)(2,1)}, bf16[3,640,128]{2,1,0:T(8,128)(2,1)}, u32[]{:S(2)}, u32[]{:S(2)}) collective-permute-start(bf16[3,640,128]{2,1,0:T(8,128)(2,1)} %fusion.30), channel_id=1, source_target_pairs={{0,16},{16,0},{1,17},{17,1},{2,18},{18,2},{3,19},{19,3},{4,20},{20... | collective-permute-start | bytes 1474568 | tf_op jit(solution)/shard_map/ppermute | solution.py:244
  346.8 7.9 %collective-permute-start.32 = (bf16[3,512,128]{2,1,0:T(8,128)(2,1)S(1)}, bf16[3,512,128]{2,1,0:T(8,128)(2,1)}, u32[]{:S(2)}, u32[]{:S(2)}) collective-permute-start(bf16[3,512,128]{2,1,0:T(8,128)(2,1)S(1)} %get-tuple-element.57), channel_id=1, source_target_pairs={{0,16},{16,0},{1,17},{17,1},{2,18},{18,2},{3,19},{19,3},{4,20},{20... | collective-permute-start | bytes 1179656 | tf_op jit(solution)/shard_map/ppermute | solution.py:227
  359.7 9.0 %collective-permute-start.37 = (bf16[3,512,128]{2,1,0:T(8,128)(2,1)}, bf16[3,512,128]{2,1,0:T(8,128)(2,1)S(1)}, u32[]{:S(2)}, u32[]{:S(2)}) collective-permute-start(bf16[3,512,128]{2,1,0:T(8,128)(2,1)} %bitcast.350), channel_id=1, source_target_pairs={{0,1},{1,2},{2,3},{4,5},{5,6},{6,7},{8,9},{9,10},{10,11},{12,13},{... | collective-permute-start | bytes 1179656 | tf_op jit(solution)/shard_map/ppermute | solution.py:182
  366.6 9.8 %collective-permute-start.36 = (bf16[3,512,128]{2,1,0:T(8,128)(2,1)S(1)}, bf16[3,512,128]{2,1,0:T(8,128)(2,1)S(1)}, u32[]{:S(2)}, u32[]{:S(2)}) collective-permute-start(bf16[3,512,128]{2,1,0:T(8,128)(2,1)S(1)} %bitcast.351), channel_id=1, source_target_pairs={{1,0},{2,1},{3,2},{5,4},{6,5},{7,6},{9,8},{10,9},{11,10},{13,12},{... | collective-permute-start | bytes 1179656 | tf_op jit(solution)/shard_map/ppermute | solution.py:183
  368.2 14.8 %copy-start.9 = (bf16[1,1,2,2,2,64,1280]{6,5,4,3,2,1,0:T(8,128)(2,1)S(1)}, bf16[1,1,2,2,2,64,1280]{6,5,4,3,2,1,0:T(8,128)(2,1)}, u32[]{:S(2)}) copy-start(bf16[1,1,2,2,2,64,1280]{6,5,4,3,2,1,0:T(8,128)(2,1)} %copy-done.8) | copy-start | bytes 3932164
  368.2 6.3 %collective-permute-start.33 = (bf16[2,2,64,384]{3,2,1,0:T(8,128)(2,1)S(1)}, bf16[2,2,64,384]{3,2,1,0:T(8,128)(2,1)S(1)}, u32[]{:S(2)}, u32[]{:S(2)}) collective-permute-start(bf16[2,2,64,384]{3,2,1,0:T(8,128)(2,1)S(1)} %bitcast.338), channel_id=1, source_target_pairs={{16,0},{0,16},{17,1},{1,17},{18,2},{2,18},{19,3},{3,19},{20,4},{4,... | collective-permute-start | bytes 589832 | tf_op jit(solution)/shard_map/ppermute | solution.py:18
  368.7 9.8 %collective-permute-start.38 = (bf16[3,512,128]{2,1,0:T(8,128)(2,1)S(1)}, bf16[3,512,128]{2,1,0:T(8,128)(2,1)S(1)}, u32[]{:S(2)}, u32[]{:S(2)}) collective-permute-start(bf16[3,512,128]{2,1,0:T(8,128)(2,1)S(1)} %collective-permute-done.37), channel_id=1, source_target_pairs={{0,1},{1,2},{2,3},{4,5},{5,6},{6,7},{8,9},{9,10},{10,11},{12,13},{... | collective-permute-start | bytes 1179656 | tf_op jit(solution)/shard_map/ppermute | solution.py:182
  374.6 9.3 %collective-permute-start.34 = (bf16[2,2,64,384]{3,2,0,1:T(8,128)(2,1)S(1)}, bf16[2,2,64,384]{3,2,0,1:T(8,128)(2,1)S(1)}, u32[]{:S(2)}, u32[]{:S(2)}) collective-permute-start(bf16[2,2,64,384]{3,2,0,1:T(8,128)(2,1)S(1)} %get-tuple-element.88), channel_id=1, source_target_pairs={{8,0},{12,4},{0,8},{4,12},{9,1},{13,5},{1,9},{5,13},{10,2},{14,6},... | collective-permute-start | bytes 589832 | tf_op jit(solution)/shard_map/ppermute | solution.py:18
  376.4 9.7 %collective-permute-start.40 = (bf16[3,512,128]{2,1,0:T(8,128)(2,1)S(1)}, bf16[3,512,128]{2,1,0:T(8,128)(2,1)S(1)}, u32[]{:S(2)}, u32[]{:S(2)}) collective-permute-start(bf16[3,512,128]{2,1,0:T(8,128)(2,1)S(1)} %collective-permute-done.36), channel_id=1, source_target_pairs={{1,0},{2,1},{3,2},{5,4},{6,5},{7,6},{9,8},{10,9},{11,10},{13,12},{... | collective-permute-start | bytes 1179656 | tf_op jit(solution)/shard_map/ppermute | solution.py:183
  378.5 9.7 %collective-permute-start.39 = (bf16[3,512,128]{2,1,0:T(8,128)(2,1)S(1)}, bf16[3,512,128]{2,1,0:T(8,128)(2,1)S(1)}, u32[]{:S(2)}, u32[]{:S(2)}) collective-permute-start(bf16[3,512,128]{2,1,0:T(8,128)(2,1)S(1)} %collective-permute-done.38), channel_id=1, source_target_pairs={{0,1},{1,2},{2,3},{4,5},{5,6},{6,7},{8,9},{9,10},{10,11},{12,13},{... | collective-permute-start | bytes 1179656 | tf_op jit(solution)/shard_map/ppermute | solution.py:182
  383.9 18.2 %collective-permute-start.35 = (bf16[2,2,64,384]{3,2,1,0:T(8,128)(2,1)S(1)}, bf16[2,2,64,384]{3,2,1,0:T(8,128)(2,1)S(1)}, u32[]{:S(2)}, u32[]{:S(2)}) collective-permute-start(bf16[2,2,64,384]{3,2,1,0:T(8,128)(2,1)S(1)} %get-tuple-element.86), channel_id=1, source_target_pairs={{4,0},{0,4},{12,8},{8,12},{5,1},{1,5},{13,9},{9,13},{6,2},{2,6},{1... | collective-permute-start | bytes 589832 | tf_op jit(solution)/shard_map/ppermute | solution.py:18
  386.1 11.3 %collective-permute-start.41 = (bf16[3,512,128]{2,1,0:T(8,128)(2,1)S(1)}, bf16[3,512,128]{2,1,0:T(8,128)(2,1)S(1)}, u32[]{:S(2)}, u32[]{:S(2)}) collective-permute-start(bf16[3,512,128]{2,1,0:T(8,128)(2,1)S(1)} %collective-permute-done.40), channel_id=1, source_target_pairs={{1,0},{2,1},{3,2},{5,4},{6,5},{7,6},{9,8},{10,9},{11,10},{13,12},{... | collective-permute-start | bytes 1179656 | tf_op jit(solution)/shard_map/ppermute | solution.py:183
  399.2 11.8 %collective-permute-start.42 = (bf16[3,640,128]{2,1,0:T(8,128)(2,1)}, bf16[3,640,128]{2,1,0:T(8,128)(2,1)}, u32[]{:S(2)}, u32[]{:S(2)}) collective-permute-start(bf16[3,640,128]{2,1,0:T(8,128)(2,1)} %fusion.31), channel_id=1, source_target_pairs={{0,16},{16,0},{1,17},{17,1},{2,18},{18,2},{3,19},{19,3},{4,20},{20... | collective-permute-start | bytes 1474568 | tf_op jit(solution)/shard_map/ppermute | solution.py:244
  (16 other events, 86.0 us)
Sparse Core Ops, SparseCore 0:
  74.4 69.8 reduce-scatter.3
  146.6 76.9 reduce-scatter.5
  226.5 72.2 reduce-scatter.7
